TPU v7x, 32 devices: a whole 2x2x4 slice. The times are simulated.
32 devices in a mesh: grp: 2 (over y), ctx: 4 (over z), head: 4 (over x, core).
Axes of the slice: x: 2, y: 2, z: 4, core: 2. Of those that a mesh axis runs over, the one named last changes fastest.
Arguments:
- main_queries: bfloat16 [1024, 128, 576], P(('grp', 'ctx'), 'head'), parts along dimension 0, may hold values from -6 to 6
- latent_keys: bfloat16 [32768, 576], P(('grp', 'ctx')), parts along dimension 0, may hold values from -6 to 6
- lse: float32 [1024, 128], P(('grp', 'ctx'), 'head'), parts along dimension 0, may hold values from 6 to 10
- index_queries: bfloat16 [1024, 64, 128], P(('grp', 'ctx'), 'head'), parts along dimension 0, may hold values from -9 to 9
- index_keys: bfloat16 [32768, 128], P(('grp', 'ctx')), parts along dimension 0, may hold values from -1 to 1
- head_weights: float32 [1024, 64], P(('grp', 'ctx'), 'head'), parts along dimension 0, may hold values from -0.1 to 0.5
- loss_cotangent: float32 [1024], P(('grp', 'ctx')), parts along dimension 0, may hold values from 32 to 128
- block_ids: int32 [1024, 32], P(('grp', 'ctx')), parts along dimension 0, may hold values from 0 to 255, as said below
Outputs:
- d_index_queries: bfloat16 [1024, 64, 128], P(('grp', 'ctx'), 'head'), parts along dimension 0
- d_head_weights: float32 [1024, 64], P(('grp', 'ctx'), 'head'), parts along dimension 0
- d_index_keys: float32 [32768, 128], P(('grp', 'ctx')), parts along dimension 0
There are 2 independent parts, one for each index of `grp`. A program takes and returns all parts, laid end to end along the dimension named above; each array names one. Nothing has to cross between parts.
Inputs may be any that keep to these rules, and one draw needn't show every extreme that they name: `block_ids`: each row names 32 different blocks, none of which starts after the query's position. The 128 rows of one ctx device name exactly 64 distinct blocks together; at most 32 of them lie among the keys of any one ctx device, and exactly 32 among the keys of the last ctx device.
All inputs are finite; a program needn't handle non-finite values.
Results may differ from a plain program's by a relative error of at most 0.0048.
Values may be sent and summed in bfloat16 or wider, within the bound.
A program may use at most 192 MiB of HBM per device.

v0:
```python
import jax
import jax.numpy as jnp
from jax import lax
from jax.sharding import PartitionSpec as P

BLK = 64
UB = 64


ATTN_SCALE = 192.0 ** (-0.5)


def smooth_gate(value):
    return jnp.maximum(value, 0.0)


def smooth_slope(value):
    return jnp.where(value > 0.0, 1.0, 0.0)


def body(
    main_queries,
    latent_keys,
    lse,
    index_queries,
    index_keys,
    head_weights,
    loss_cotangent,
    block_ids,
):
    ctx_count = lax.axis_size("ctx")
    ctx_rank = lax.axis_index("ctx")
    query_rows = main_queries.shape[0]
    key_rows = latent_keys.shape[0]
    width_lat = latent_keys.shape[1]
    width_idx = index_keys.shape[1]
    owner_blocks = key_rows // BLK
    slot_count = 2 * UB // ctx_count
    all_blocks = owner_blocks * ctx_count
    present = jnp.zeros((all_blocks,), jnp.int32).at[block_ids.reshape(-1)].max(1)
    owner_grid = present.reshape(ctx_count, owner_blocks)
    slot_order = jnp.cumsum(owner_grid, axis=1) - 1
    filled = jnp.sum(owner_grid, axis=1)
    slot_iota = jnp.arange(slot_count, dtype=jnp.int32)
    block_iota = jnp.arange(owner_blocks, dtype=jnp.int32)
    slot_match = (owner_grid[:, :, None] == 1) & (
        slot_order[:, :, None] == slot_iota[None, None, :]
    )
    wanted = jnp.sum(jnp.where(slot_match, block_iota[None, :, None], 0), axis=1)
    used_slots = slot_iota[None, :] < filled[:, None]
    asked_for = lax.all_to_all(wanted, "ctx", split_axis=0, concat_axis=0, tiled=True)
    lat_local = latent_keys.reshape(owner_blocks, BLK, width_lat)
    idx_local = index_keys.reshape(owner_blocks, BLK, width_idx)
    lat_got, idx_got = (
        lax.all_to_all(lat_local[asked_for], "ctx", split_axis=0, concat_axis=0, tiled=True),
        lax.all_to_all(idx_local[asked_for], "ctx", split_axis=0, concat_axis=0, tiled=True),
    )
    union_slots = ctx_count * slot_count
    used_flat = used_slots.reshape(-1).astype(jnp.int32)
    compact_pos = jnp.cumsum(used_flat) - 1
    union_iota = jnp.arange(UB, dtype=jnp.int32)
    flat_iota = jnp.arange(union_slots, dtype=jnp.int32)
    compact_hit = (used_flat[None, :] == 1) & (compact_pos[None, :] == union_iota[:, None])
    source = jnp.sum(jnp.where(compact_hit, flat_iota[None, :], 0), axis=1)
    global_block = flat_iota // slot_count * owner_blocks + wanted.reshape(-1)
    union_block = global_block[source]
    lat_keys = lat_got.reshape(union_slots, BLK, width_lat)[source].reshape(UB * BLK, width_lat)
    idx_keys = idx_got.reshape(union_slots, BLK, width_idx)[source].reshape(UB * BLK, width_idx)
    chosen = jnp.any(block_ids[:, :, None] == union_block[None, None, :], axis=1)
    key_pos = union_block[:, None] * BLK + jnp.arange(BLK, dtype=jnp.int32)[None, :]
    query_pos = (
        all_blocks * BLK
        - query_rows * ctx_count
        + ctx_rank * query_rows
        + jnp.arange(query_rows, dtype=jnp.int32)
    )
    visible = (chosen[:, :, None] & (key_pos[None, :, :] <= query_pos[:, None, None])).reshape(
        query_rows, UB * BLK
    )
    group_rows = min(UB, max(1, 512 // BLK)) * BLK
    groups = UB * BLK // group_rows

    def head_mass(group_pair):
        group_keys, group_vis = group_pair
        scores = (
            jnp.einsum("qhc,sc->qhs", main_queries, group_keys, preferred_element_type=jnp.float32)
            * ATTN_SCALE
        )
        main_prob = jnp.where(group_vis[:, None, :], jnp.exp(scores - lse[:, :, None]), 0.0)
        return jnp.sum(main_prob, axis=1)

    mass_groups = lax.map(
        head_mass,
        (
            lat_keys.reshape(groups, group_rows, width_lat),
            visible.reshape(query_rows, groups, group_rows).transpose(1, 0, 2),
        ),
    )
    mass_part = mass_groups.transpose(1, 0, 2).reshape(query_rows, UB * BLK)
    index_pre = jnp.einsum(
        "qjc,sc->qjs", index_queries, idx_keys, preferred_element_type=jnp.float32
    )
    activated = smooth_gate(index_pre)
    score_part = jnp.einsum("qj,qjs->qs", head_weights, activated, precision=lax.Precision.HIGHEST)
    mass_whole, score_whole = lax.psum((mass_part, score_part), "head")
    row_top = jnp.max(jnp.where(visible, score_whole, -1e30), axis=1)
    exponent = jnp.where(visible, jnp.exp(score_whole - row_top[:, None]), 0.0)
    index_prob = exponent / jnp.sum(exponent, axis=1, keepdims=True)
    score_grad = loss_cotangent[:, None] * (
        index_prob - mass_whole / jnp.sum(mass_whole, axis=1, keepdims=True)
    )
    d_weights = jnp.einsum("qs,qjs->qj", score_grad, activated, precision=lax.Precision.HIGHEST)
    pre_grad = (score_grad[:, None, :] * head_weights[:, :, None] * smooth_slope(index_pre)).astype(
        jnp.bfloat16
    )
    d_queries = jnp.einsum(
        "qjs,sc->qjc", pre_grad, idx_keys, preferred_element_type=jnp.float32
    ).astype(jnp.bfloat16)
    key_grad = jnp.einsum(
        "qjs,qjc->sc", pre_grad, index_queries, preferred_element_type=jnp.float32
    )
    spread = (source[:, None] == flat_iota[None, :]).astype(jnp.float32)
    slotted = jnp.einsum(
        "uf,ukc->fkc", spread, key_grad.reshape(UB, BLK, width_idx), precision=lax.Precision.HIGHEST
    ).reshape(ctx_count, slot_count, BLK, width_idx)
    landing = (asked_for.reshape(-1)[:, None] == block_iota[None, :]).astype(jnp.float32)
    returned = lax.all_to_all(slotted, "ctx", split_axis=0, concat_axis=0, tiled=True)
    owner_sum = jnp.einsum(
        "fb,fkc->bkc",
        landing,
        returned.reshape(union_slots, BLK, width_idx),
        precision=lax.Precision.HIGHEST,
    )
    d_keys = lax.psum(owner_sum, "head").reshape(key_rows, width_idx)
    return (d_queries, d_weights, d_keys)


def solution(mesh):
    placed = (
        P(("grp", "ctx"), "head", None),
        P(("grp", "ctx"), None),
        P(("grp", "ctx"), "head"),
        P(("grp", "ctx"), "head", None),
        P(("grp", "ctx"), None),
        P(("grp", "ctx"), "head"),
        P(("grp", "ctx")),
        P(("grp", "ctx"), None),
    )
    return jax.shard_map(
        body,
        mesh=mesh,
        in_specs=placed,
        out_specs=(
            P(("grp", "ctx"), "head", None),
            P(("grp", "ctx"), "head"),
            P(("grp", "ctx"), None),
        ),
        check_vma=False,
    )
```

profile of v0, /device:TPU:0, one launch (start us, length us, event | category | flops | bytes accessed | tf_op | source)
XLA Modules:
  0.0 702.5 jit_solution(9329928714834282022)
XLA Ops:
  7.2 0.9 copy.46
  8.2 28.8 %scatter_custom_fusion = s32[256]{0:T(256)S(1)} fusion(s32[4096]{0:T(1024)S(1)} %bitcast.115, s32[4096]{0:T(1024)S(1)} %broadcast.182, s32[]{:T(128)} %constant.31.clone.1), kind=kCustom, calls=%fused_computation.71 | custom fusion | flops 4096 | bytes 1028 | tf_op jit(solution)/shard_map/scatter-max | solution.py:40
  37.1 0.2 reduce_window_sum.18
  37.5 11.7 %all_to_all.27 = s32[4,1,32]{2,1,0:T(1,128)S(1)} all-to-all(s32[4,1,32]{2,1,0:T(1,128)S(1)} %bitcast.113), channel_id=1, replica_groups=mesh['grp'=2,'ctx'=4,'head'=4] {'ctx'}, dimensions={0} | all-to-all | bytes 1024 | tf_op jit(solution)/shard_map/all_to_all | solution.py:51
  49.3 2.1 gather_fusion.1
  51.4 3.6 all-to-all-start.1
  55.0 7.7 %copy.50 = bf16[4096,576]{1,0:T(8,128)(2,1)} copy(bf16[4096,576]{0,1:T(8,128)(2,1)} %param.11) | data formatting | bytes 9437184 | tf_op args[1]
  62.7 9.9 %gather_fusion.3 = bf16[128,64,576]{2,1,0:T(8,128)(2,1)} fusion(bf16[64,64,576]{2,1,0:T(8,128)(2,1)} %bitcast.102, s32[1024]{0:T(1024)S(1)} %pad_clamp_fusion), kind=kCustom, calls=%fused_computation.3 | custom fusion | bytes 18874880 | tf_op jit(solution)/shard_map/gather | solution.py:55
  72.6 29.5 %all-to-all-done.1 = bf16[4,32,64,128]{3,2,1,0:T(8,128)(2,1)S(1)} async-done(((bf16[4,32,64,128]{3,2,1,0:T(8,128)(2,1)}), bf16[4,32,64,128]{3,2,1,0:T(8,128)(2,1)S(1)}, u32[]{:S(2)}, u32[]{:S(2)}) %all-to-all-start.1) | async-done | bytes 2097184 | tf_op jit(solution)/shard_map/all_to_all | solution.py:56
  102.0 6.1 all-to-all-start.2
  108.1 0.2 all-reduce.6.cloned.1.call-start
  108.9 0.2 reduce-window.8
  109.3 0.8 gather_fusion
  110.3 0.2 compare_reduce_fusion
  110.7 1.4 fusion.12
  112.1 0.7 gather_fusion.2
  112.9 15.8 %fusion.6 = (f32[128,4096]{0,1:T(8,128)}, f32[4096,128,16]{1,0,2:T(8,128)}) fusion(f32[128,16]{0,1:T(8,128)S(1)} %copy-done.9, bf16[4096,128,1]{1,0,2:T(8,128)(2,1)S(1)} %bitcast.108, bf16[128,16,128]{2,1,0:T(8,128)(2,1)} %param.13), kind=kOutput, calls=%fused_computation.18 | convolution fusion | flops 2172125184 | bytes 37232640 | tf_op jit(solution)/shard_map/qjc,sc->qjs/dot_general | solution.py:100
  128.7 207.0 %all-to-all-done.2 = bf16[4,32,64,576]{3,2,1,0:T(8,128)(2,1)} async-done(((bf16[4,32,64,576]{3,2,1,0:T(8,128)(2,1)}), bf16[4,32,64,576]{3,2,1,0:T(8,128)(2,1)}, u32[]{:S(2)}, u32[]{:S(2)}) %all-to-all-start.2) | async-done | bytes 9437216 | tf_op jit(solution)/shard_map/all_to_all | solution.py:55
  335.6 7.5 %gather_fusion.4 = bf16[64,64,576]{2,1,0:T(8,128)(2,1)} fusion(bf16[128,64,576]{2,1,0:T(8,128)(2,1)} %bitcast.23, s32[1024]{0:T(1024)S(1)} %pad_clamp_fusion.1), kind=kCustom, calls=%fused_computation.4 | custom fusion | bytes 9437440 | tf_op jit(solution)/shard_map/gather | solution.py:67
  343.1 7.7 %copy.51 = bf16[8,512,576]{1,2,0:T(8,128)(2,1)} copy(bf16[8,512,576]{2,1,0:T(8,128)(2,1)} %bitcast.104) | data formatting | bytes 9437184 | tf_op jit(solution)/shard_map/while | solution.py:92
  350.8 68.4 %while.10 = (s32[]{:T(128)}, f32[8,128,512]{1,2,0:T(8,128)}, pred[8,128,512]{1,2,0:T(8,128)(4,1)}, bf16[8,512,576]{1,2,0:T(8,128)(2,1)}, bf16[128,32,576]{0,2,1:T(8,128)(2,1)}, /*index=5*/f32[128,32]{0,1:T(8,128)S(1)}, s32[]{:T(128)}) while((s32[]{:T(128)}, f32[8,128,512]{1,2,0:T(8,128)}, pred[8,128,512]{1,2,0:T(8,128)(4,1)}, ...), condition=%wide.region_12.13_spmd, body=%wide.region_10.12_spmd.sunk | while | flops 2424242176 | bytes 6307937 | solution.py:92
  350.8 0.8 dynamic-slice_bitcast_fusion.2
  351.7 7.0 fusion.43
  358.7 0.7 bitcast_dynamic-update-slice_fusion.2
  359.4 0.8 dynamic-slice_bitcast_fusion.2
  360.2 7.0 fusion.43
  367.2 0.7 bitcast_dynamic-update-slice_fusion.2
  367.9 0.8 dynamic-slice_bitcast_fusion.2
  368.8 7.0 fusion.43
  375.8 0.7 bitcast_dynamic-update-slice_fusion.2
  376.5 0.8 dynamic-slice_bitcast_fusion.2
  377.3 7.0 fusion.43
  384.3 0.7 bitcast_dynamic-update-slice_fusion.2
  385.1 0.8 dynamic-slice_bitcast_fusion.2
  385.9 7.0 fusion.43
  392.9 0.7 bitcast_dynamic-update-slice_fusion.2
  393.6 0.8 dynamic-slice_bitcast_fusion.2
  394.5 7.0 fusion.43
  401.4 0.7 bitcast_dynamic-update-slice_fusion.2
  402.2 0.8 dynamic-slice_bitcast_fusion.2
  403.0 7.0 fusion.43
  410.0 0.7 bitcast_dynamic-update-slice_fusion.2
  410.7 0.8 dynamic-slice_bitcast_fusion.2
  411.6 7.0 fusion.43
  418.5 0.7 bitcast_dynamic-update-slice_fusion.2
  419.5 84.7 %all-reduce.6.cloned.1.call-done = (f32[128,4096]{0,1:T(8,128)}, f32[128,4096]{0,1:T(8,128)}) async-done(((f32[128,4096]{0,1:T(8,128)}, f32[128,4096]{0,1:T(8,128)}), (f32[128,4096]{0,1:T(8,128)}, f32[128,4096]{0,1:T(8,128)})) %all-reduce.6.cloned.1.call-update) | async-done | bytes 4194320 | tf_op jit(solution)/shard_map/psum | solution.py:105
  504.2 2.1 select_reduce_fusion
  506.3 2.0 fusion.13
  508.3 2.2 reduce_sum.61
  510.5 2.9 subtract_multiply_fusion
  513.4 14.2 %fusion.14 = f32[4096,128,1]{1,0,2:T(8,128)S(1)} fusion(bf16[128,16,128]{2,1,0:T(8,128)(2,1)S(1)} %copy-done.7, f32[4096,128,16]{1,0,2:T(8,128)} %get-tuple-element.83, f32[128,16]{0,1:T(8,128)S(1)} %copy-done.9, f32[128,4096]{0,1:T(8,128)S(1)} %subtract_multiply_fusion), kind=kOutput, calls=%fused_computation.33 | convolution fusion | flops 2189426688 | bytes 38281216 | tf_op jit(solution)/shard_map/qjs,qjc->sc/dot_general | solution.py:119
  527.7 5.1 fusion.9
  532.8 5.1 all-to-all-start.3
  537.9 0.5 broadcast.216
  538.5 0.7 reduce.9
  539.2 13.2 %convolution_convert_fusion = bf16[128,16,128]{2,0,1:T(8,128)(2,1)S(1)} fusion(bf16[4096,128,1]{1,0,2:T(8,128)(2,1)S(1)} %bitcast.109, f32[4096,128,16]{1,0,2:T(8,128)} %get-tuple-element.83, f32[128,16]{0,1:T(8,128)S(1)} %copy-done.9, f32[128,4096]{0,1:T(8,128)S(1)} %copy-done.4), kind=kOutput, calls=%fused_computation.31 | convolution fusion | flops 2189688832 | bytes 37232640 | tf_op jit(solution)/shard_map/qjs,sc->qjc/dot_general | solution.py:116
  552.5 1.1 copy.58
  553.6 77.6 %all-to-all-done.3 = f32[4,32,64,128]{3,1,2,0:T(8,128)} async-done(((f32[4,32,64,128]{3,1,2,0:T(8,128)}), f32[4,32,64,128]{3,1,2,0:T(8,128)}, u32[]{:S(2)}, u32[]{:S(2)}) %all-to-all-start.3) | async-done | bytes 4194336 | tf_op jit(solution)/shard_map/all_to_all | solution.py:127
  631.2 4.6 copy.55
  635.9 4.2 fusion.7
  640.0 2.5 copy.57
  642.6 13.5 %fusion.4 = f32[128,16]{0,1:T(8,128)} fusion(f32[4096,128,16]{1,0,2:T(8,128)} %get-tuple-element.83, f32[128,4096]{0,1:T(8,128)S(1)} %copy-done.4), kind=kLoop, calls=%fused_computation.14 | loop fusion | flops 25163776 | bytes 35659776 | tf_op jit(solution)/shard_map/qs,qjs->qj/dot_general | solution.py:112
  656.1 36.6 %all-reduce.4.cloned.1.call-done = f32[4096,128]{1,0:T(8,128)} async-done(((f32[4096,128]{1,0:T(8,128)}), f32[4096,128]{1,0:T(8,128)}) %all-reduce.4.cloned.1.call-update) | async-done | bytes 2097168 | tf_op jit(solution)/shard_map/psum | solution.py:134
  692.6 3.0 copy.94
  (62 shorter events, 1.9 us)
Async XLA Ops:
  7.2 42.1 %copy-start = (bf16[4096,128]{1,0:T(8,128)(2,1)S(1)}, bf16[4096,128]{1,0:T(8,128)(2,1)}, u32[]{:S(2)}) copy-start(bf16[4096,128]{1,0:T(8,128)(2,1)} %param.14) | copy-start | bytes 3145732
  51.4 50.6 %all-to-all-start.1 = ((bf16[4,32,64,128]{3,2,1,0:T(8,128)(2,1)}), bf16[4,32,64,128]{3,2,1,0:T(8,128)(2,1)S(1)}, u32[]{:S(2)}, u32[]{:S(2)}) async-start(bf16[4,32,64,128]{3,2,1,0:T(8,128)(2,1)} %bitcast.14), calls=%async_computation.1 | async-start | bytes 4194304 | tf_op jit(solution)/shard_map/all_to_all | solution.py:56
  102.0 8.3 %copy-start.8 = (s32[128,32]{0,1:T(8,128)S(1)}, s32[128,32]{0,1:T(8,128)}, u32[]{:S(2)}) copy-start(s32[128,32]{0,1:T(8,128)} %param.17) | copy-start | bytes 49156
  102.0 233.6 %all-to-all-start.2 = ((bf16[4,32,64,576]{3,2,1,0:T(8,128)(2,1)}), bf16[4,32,64,576]{3,2,1,0:T(8,128)(2,1)}, u32[]{:S(2)}, u32[]{:S(2)}) async-start(bf16[4,32,64,576]{3,2,1,0:T(8,128)(2,1)} %bitcast.103), calls=%async_computation.2 | async-start | bytes 20971520 | tf_op jit(solution)/shard_map/all_to_all | solution.py:55
  108.1 4.7 copy-start.9
  108.1 396.1 %all-reduce.6.cloned.1.call-start = ((), (), s32[]{:S(2)}) async-start(), calls=%async_computation.5 | async-start | bytes 8388608 | tf_op jit(solution)/shard_map/psum | solution.py:105
  112.8 15.8 %copy-start.5 = (bf16[64,64,128]{2,1,0:T(8,128)(2,1)}, bf16[64,64,128]{2,1,0:T(8,128)(2,1)S(1)}, u32[]{:S(2)}) copy-start(bf16[64,64,128]{2,1,0:T(8,128)(2,1)S(1)} %gather_fusion.2) | copy-start | bytes 3145732
  343.1 7.7 %copy-start.11 = (f32[128,32]{0,1:T(8,128)S(1)}, f32[128,32]{0,1:T(8,128)}, u32[]{:S(2)}) copy-start(f32[128,32]{0,1:T(8,128)} %param.12) | copy-start | bytes 49156
  419.3 91.2 %copy-start.10 = (f32[128]{0:T(128)S(1)}, f32[128]{0:T(128)}, u32[]{:S(2)}) copy-start(f32[128]{0:T(128)} %param.16) | copy-start | bytes 1540
  504.2 6.3 copy-start.2
  508.3 5.2 copy-start.7
  513.4 14.3 %copy-start.3 = (f32[128,4096]{0,1:T(8,128)}, f32[128,4096]{0,1:T(8,128)S(1)}, u32[]{:S(2)}) copy-start(f32[128,4096]{0,1:T(8,128)S(1)} %subtract_multiply_fusion) | copy-start | bytes 6291460
  532.8 6.4 copy-start.4
  532.8 6.4 copy-start.6
  532.8 98.5 %all-to-all-start.3 = ((f32[4,32,64,128]{3,1,2,0:T(8,128)}), f32[4,32,64,128]{3,1,2,0:T(8,128)}, u32[]{:S(2)}, u32[]{:S(2)}) async-start(f32[4,32,64,128]{3,1,2,0:T(8,128)} %fusion.9), calls=%async_computation.3 | async-start | bytes 8388608 | tf_op jit(solution)/shard_map/all_to_all | solution.py:127
  537.9 154.8 %all-reduce.4.cloned.1.call-start = ((), (), s32[]{:S(2)}) async-start(), calls=%async_computation.4 | async-start | bytes 4194304 | tf_op jit(solution)/shard_map/psum | solution.py:134
  642.6 53.1 %copy-start.1 = (bf16[4096,128]{1,0:T(8,128)(2,1)S(1)}, bf16[4096,128]{1,0:T(8,128)(2,1)}, u32[]{:S(2)}) copy-start(bf16[4096,128]{1,0:T(8,128)(2,1)} %param.14) | copy-start | bytes 3145732
Sparse Core Ops, SparseCore 0:
  419.4 84.7 all-reduce.5
  642.7 49.9 all-reduce.3
where the time goes:
time: 704 us; the launch traced here: 703 us
  waiting for transfers between devices  435 us (62%)
  matrix products  108 us (15%)
  local copies, waits for them, and re-layouts  62.9 us (9%)
  other arithmetic  54.8 us (8%)
  starting transfers between devices  15.1 us (2%)
  between operations  14.3 us (2%)
  blocking collectives  11.7 us (2%)
    all_to_all x1, waiting for transfers between devices, body(): lax.all_to_all(lat_local[asked_for], 'ctx', split_axis=0, concat_axis=0,...  207 us
    psum x1, waiting for transfers between devices, body(): mass_whole, score_whole = lax.psum((mass_part, score_part), 'head')  84.7 us
    all_to_all x1, waiting for transfers between devices, body(): lax.all_to_all(slotted, 'ctx', split_axis=0, concat_axis=0, tiled=True)  77.6 us
    dot_general x8, matrix products, head_mass(): jnp.einsum('qhc,sc->qhs', main_queries, group_keys, preferred_element_typ...  55.8 us
    psum x1, waiting for transfers between devices, body(): d_keys = lax.psum(owner_sum, 'head').reshape(key_rows, width_idx)  36.6 us
    all_to_all x1, waiting for transfers between devices, body(): lax.all_to_all(idx_local[asked_for], 'ctx', split_axis=0, concat_axis=0,...  29.5 us
    another operation x1, other arithmetic, body(): jnp.zeros((all_blocks,), jnp.int32).at[block_ids.reshape(-1)].max(1)  28.8 us
    dot_general x1, matrix products, body(): jnp.einsum('qjc,sc->qjs', index_queries, idx_keys, preferred_element_type...  15.8 us
  transfers between devices with their start and end apart: 5, of which 5 were waited for; matrix products, arithmetic and copies ran while one was open for 10% of the time, Pallas kernels for 0%

commit v1 on v0

v1 whole, which is shorter than its diff:
```python
import functools
import math

import jax
import jax.numpy as jnp
from jax import lax
from jax.experimental import pallas as pl
from jax.experimental.pallas import tpu as pltpu
from jax.sharding import PartitionSpec as P

BLK = 64
UB = 64
GB = 8
ATTN_SCALE = 192.0 ** (-0.5)
LOG2E = math.log2(math.e)
MESH = pl.DeviceIdType.MESH
VMEM_LIMIT = 56 * 1024 * 1024
F32 = jnp.float32
BF16 = jnp.bfloat16


def place():
    head = lax.axis_index("head")
    x, core = head // 2, lax.rem(head, 2)
    return head, x, core, x * 2 + 1 - core


def greet(peers):
    barrier = pltpu.get_barrier_semaphore()
    for peer in peers:
        pl.semaphore_signal(barrier, inc=1, device_id=peer, device_id_type=MESH)
    pl.semaphore_wait(barrier, len(peers))


def remote(src, dst, send, recv, peer):
    return pltpu.make_async_remote_copy(
        src_ref=src, dst_ref=dst, send_sem=send, recv_sem=recv,
        device_id=peer, device_id_type=MESH,
    )


def fetch_kernel(n_ctx, n_head, lat_mine, idx_mine, lat_own, idx_own, lat_got, idx_got,
                 own_sem, recv_sem, s_ctx, s_x, s_core):
    me = lax.axis_index("ctx")
    head, x, core, partner = place()
    n_x = n_head // 2
    others = [lax.rem(me + k, n_ctx) for k in range(1, n_ctx)]
    xs = [lax.rem(x + k, n_x) for k in range(1, n_x)]
    greet([{"ctx": o} for o in others] + [{"head": v * 2 + core} for v in xs] + [{"head": partner}])
    mine, own, got = (idx_mine, lat_mine), (idx_own, lat_own), (idx_got, lat_got)
    pending = []
    for a in range(2):
        for i, o in enumerate(others):
            c = remote(mine[a].at[o], got[a].at[me, head], s_ctx.at[a, i],
                       recv_sem.at[a, me, head], {"ctx": o})
            c.start()
            pending.append(c)
    locals_ = []
    for a in range(2):
        c = pltpu.make_async_copy(own[a], got[a].at[me], own_sem.at[a])
        c.start()
        locals_.append(c)

    def arrived(a, o, h):
        remote(got[a].at[o, h], got[a].at[o, h], s_core.at[a, 0, 0], recv_sem.at[a, o, h],
               {"head": partner}).wait_recv()

    def forward(a, i, o, h, slot):
        c = remote(got[a].at[o, h], got[a].at[o, h], s_core.at[a, i, slot],
                   recv_sem.at[a, o, h], {"head": partner})
        c.start()
        pending.append(c)

    sources = [lax.rem(me + n_ctx - k, n_ctx) for k in range(1, n_ctx)]
    for a in range(2):
        for i, o in enumerate(sources):
            arrived(a, o, head)
            for j, v in enumerate(xs):
                c = remote(got[a].at[o, head], got[a].at[o, head], s_x.at[a, i, j],
                           recv_sem.at[a, o, head], {"head": v * 2 + core})
                c.start()
                pending.append(c)
            forward(a, i, o, head, 0)
    for a in range(2):
        for i, o in enumerate(sources):
            for j, v in enumerate(xs):
                arrived(a, o, v * 2 + core)
                forward(a, i, o, v * 2 + core, 1 + j)
    for a in range(2):
        for i, o in enumerate(sources):
            for v in [x] + xs:
                arrived(a, o, v * 2 + 1 - core)
    for c in pending:
        c.wait_send()
    for c in locals_:
        c.wait()


def fetch(n_ctx, n_head, lat_mine, idx_mine, lat_own, idx_own):
    per, _, wl = lat_mine.shape[1:]
    wi = idx_mine.shape[-1]
    n_x = n_head // 2
    dma = pltpu.SemaphoreType.DMA
    return pl.pallas_call(
        functools.partial(fetch_kernel, n_ctx, n_head),
        out_shape=(
            jax.ShapeDtypeStruct((n_ctx, n_head, per, BLK, wl), BF16),
            jax.ShapeDtypeStruct((n_ctx, n_head, per, BLK, wi), BF16),
        ),
        in_specs=[pl.BlockSpec(memory_space=pl.ANY)] * 4,
        out_specs=(pl.BlockSpec(memory_space=pl.ANY),) * 2,
        scratch_shapes=[
            dma((2,)),
            dma((2, n_ctx, n_head)),
            dma((2, n_ctx)),
            dma((2, n_ctx, n_x)),
            dma((2, n_ctx, n_x)),
        ],
        compiler_params=pltpu.CompilerParams(collective_id=0, has_side_effects=True),
        name="fetch",
    )(lat_mine, idx_mine, lat_own, idx_own)


def nt(a, b):
    return lax.dot_general(a, b, (((1,), (1,)), ((), ())), preferred_element_type=F32)


def forward_kernel(src, *refs):
    lat = refs[:GB]
    idx = refs[GB:2 * GB]
    mq, lse, iq, hw, lim, mass, score, keys, ikeys = refs[2 * GB:]
    q = mass.shape[1]
    for b in range(GB):
        keys[b * BLK:(b + 1) * BLK, :] = lat[b][0]
        ikeys[b * BLK:(b + 1) * BLK, :] = idx[b][0]
    mass[...] = jnp.zeros_like(mass)
    score[...] = jnp.zeros_like(score)

    def main(i, carry):
        s = nt(keys[...], mq[i])
        e = jnp.exp2(s * (ATTN_SCALE * LOG2E) - lse[pl.ds(i, 1), :])
        mass[...] += e[:, :q] + e[:, q:]
        return carry

    lax.fori_loop(0, mq.shape[0], main, 0)

    def side(i, carry):
        v = jnp.maximum(nt(ikeys[...], iq[i]), 0.0) * hw[pl.ds(i, 1), :]
        score[...] += v[:, :q] + v[:, q:]
        return carry

    lax.fori_loop(0, iq.shape[0], side, 0)
    offset = lax.broadcasted_iota(jnp.int32, (BLK, q), 0)
    for b in range(GB):
        rows = slice(b * BLK, (b + 1) * BLK)
        seen = offset <= lim[b:b + 1, :]
        mass[rows, :] = jnp.where(seen, mass[rows, :], 0.0)
        score[rows, :] = jnp.where(seen, score[rows, :], -1e30)


def slot_specs(width):
    return [
        pl.BlockSpec((1, BLK, width), lambda g, s, b=b: (s[g * GB + b], 0, 0)) for b in range(GB)
    ]


def forward(source, lat, idx, mq, lse, iq, hw, lim):
    q = lim.shape[1]
    wl, wi = lat.shape[-1], idx.shape[-1]
    rows = GB * BLK
    whole = lambda a: pl.BlockSpec(a.shape, lambda g, s, n=a.ndim: (0,) * n)
    return pl.pallas_call(
        forward_kernel,
        grid_spec=pltpu.PrefetchScalarGridSpec(
            num_scalar_prefetch=1,
            grid=(UB // GB,),
            in_specs=slot_specs(wl) + slot_specs(wi) + [whole(mq), whole(lse), whole(iq), whole(hw)]
            + [pl.BlockSpec((GB, q), lambda g, s: (g, 0))],
            out_specs=(pl.BlockSpec((rows, q), lambda g, s: (g, 0)),) * 2,
            scratch_shapes=[pltpu.VMEM((rows, wl), BF16), pltpu.VMEM((rows, wi), BF16)],
        ),
        out_shape=(jax.ShapeDtypeStruct((UB * BLK, q), F32),) * 2,
        compiler_params=pltpu.CompilerParams(vmem_limit_bytes=VMEM_LIMIT),
        name="forward",
    )(source, *([lat] * GB), *([idx] * GB), mq, lse, iq, hw, lim)


def grad_kernel(n_head, mass, score, cot, grad, got_a, part, got_b, stat, whole,
                ra, rb, rs, rg, sa, sb, ss, sg):
    head, x, core, partner = place()
    n_x = n_head // 2
    span = mass.shape[0] // n_head
    xs = [lax.rem(x + k, n_x) for k in range(1, n_x)]
    heads = [lax.rem(head + k, n_head) for k in range(1, n_head)]
    greet([{"head": h} for h in heads])
    rows = lambda h: pl.ds(pl.multiple_of(h * span, span), span)
    both = (score, mass)
    pending = []
    order = xs + [x]
    for v in order:
        for a in range(2):
            c = remote(both[a].at[rows(v * 2 + 1 - core)], got_a.at[a, v], sa.at[a, v],
                       ra.at[a, v], {"head": partner})
            c.start()
            pending.append(c)
    for i, v in enumerate(order):
        for a in range(2):
            remote(got_a.at[a, v], got_a.at[a, v], sa.at[a, v], ra.at[a, v],
                   {"head": partner}).wait_recv()
            part[a, v] = both[a][rows(v * 2 + core), :] + got_a[a, v]
            if i < n_x - 1:
                c = remote(part.at[a, v], got_b.at[a, x], sb.at[a, v], rb.at[a, x],
                           {"head": v * 2 + core})
                c.start()
                pending.append(c)
    for v in xs:
        for a in range(2):
            remote(got_b.at[a, v], got_b.at[a, v], sb.at[a, v], rb.at[a, v],
                   {"head": partner}).wait_recv()
            part[a, x] += got_b[a, v]
    top = jnp.max(part[0, x], axis=0, keepdims=True)
    expo = jnp.exp(part[0, x] - top)
    stat[head, 0:1, :] = top
    stat[head, 1:2, :] = jnp.sum(expo, axis=0, keepdims=True)
    stat[head, 2:3, :] = jnp.sum(part[1, x], axis=0, keepdims=True)
    stat[head, 3:8, :] = jnp.zeros((5, top.shape[1]), F32)
    for i, h in enumerate(heads):
        c = remote(stat.at[head], stat.at[head], ss.at[i], rs.at[head], {"head": h})
        c.start()
        pending.append(c)
    for h in heads:
        remote(stat.at[h], stat.at[h], ss.at[0], rs.at[h], {"head": partner}).wait_recv()
    best = stat[0, 0:1, :]
    for h in range(1, n_head):
        best = jnp.maximum(best, stat[h, 0:1, :])
    total = jnp.zeros_like(best)
    mass_total = jnp.zeros_like(best)
    for h in range(n_head):
        total += stat[h, 1:2, :] * jnp.exp(stat[h, 0:1, :] - best)
        mass_total += stat[h, 2:3, :]
    left = cot[...] * jnp.exp(top - best) / total
    right = cot[...] / mass_total
    whole[head] = expo * left - part[1, x] * right

    def send(h, sem, to):
        c = remote(whole.at[h], whole.at[h], sem, rg.at[h], {"head": to})
        c.start()
        pending.append(c)

    def arrived(h):
        remote(whole.at[h], whole.at[h], sg.at[0], rg.at[h], {"head": partner}).wait_recv()

    for i, v in enumerate(xs):
        send(head, sg.at[i], v * 2 + core)
    send(head, sg.at[n_x], partner)
    for i, v in enumerate(xs):
        arrived(v * 2 + core)
        send(v * 2 + core, sg.at[n_x + 1 + i], partner)
    for v in [x] + xs:
        arrived(v * 2 + 1 - core)
    for c in pending:
        c.wait_send()
    for h in range(n_head):
        grad[h * span:(h + 1) * span, :] = whole[h]


def score_grads(n_head, mass, score, cot):
    keys, q = mass.shape
    n_x, span = n_head // 2, keys // n_head
    dma = pltpu.SemaphoreType.DMA
    vm = pl.BlockSpec(memory_space=pltpu.VMEM)
    return pl.pallas_call(
        functools.partial(grad_kernel, n_head),
        out_shape=jax.ShapeDtypeStruct((keys, q), F32),
        in_specs=[vm] * 3,
        out_specs=vm,
        scratch_shapes=[
            pltpu.VMEM((2, n_x, span, q), F32),
            pltpu.VMEM((2, n_x, span, q), F32),
            pltpu.VMEM((2, n_x, span, q), F32),
            pltpu.VMEM((n_head, 8, q), F32),
            pltpu.VMEM((n_head, span, q), F32),
            dma((2, n_x)), dma((2, n_x)), dma((n_head,)), dma((n_head,)),
            dma((2, n_x)), dma((2, n_x)), dma((n_head,)), dma((n_head + 1,)),
        ],
        compiler_params=pltpu.CompilerParams(
            collective_id=1, has_side_effects=True, vmem_limit_bytes=VMEM_LIMIT
        ),
        name="score_grads",
    )(mass, score, cot)


def backward_kernel(src, *refs):
    idx = refs[:GB]
    iq, hw, grad, dq, dw, dk, ikeys, tkeys, acc, gacc = refs[GB:]
    q = grad.shape[1]
    step = pl.program_id(0)

    @pl.when(step == 0)
    def _():
        acc[...] = jnp.zeros_like(acc)
        dw[...] = jnp.zeros_like(dw)

    for b in range(GB):
        ikeys[b * BLK:(b + 1) * BLK, :] = idx[b][0]
    tkeys[...] = jnp.swapaxes(ikeys[...].astype(F32), 0, 1).astype(BF16)
    gacc[...] = jnp.zeros_like(gacc)

    def one(i, carry):
        pre = nt(ikeys[...], iq[i])
        g = jnp.concatenate([grad[...], grad[...]], axis=1)
        dw[pl.ds(i, 1), :] += jnp.sum(g * jnp.maximum(pre, 0.0), axis=0, keepdims=True)
        pg = jnp.where(pre > 0.0, g * hw[pl.ds(i, 1), :], 0.0).astype(BF16)
        acc[i] += jnp.dot(tkeys[...], pg, preferred_element_type=F32)
        gacc[...] += jnp.dot(pg, iq[i], preferred_element_type=F32)
        return carry

    lax.fori_loop(0, iq.shape[0], one, 0)
    dk[...] = gacc[...]

    @pl.when(step == pl.num_programs(0) - 1)
    def _():
        for i in range(iq.shape[0]):
            dq[i] = jnp.swapaxes(acc[i], 0, 1).astype(BF16)


def backward(source, idx, iq, hw, grad):
    q = grad.shape[1]
    wi = idx.shape[-1]
    rows = GB * BLK
    pairs = iq.shape[0]
    whole = lambda a: pl.BlockSpec(a.shape, lambda g, s, n=a.ndim: (0,) * n)
    return pl.pallas_call(
        backward_kernel,
        grid_spec=pltpu.PrefetchScalarGridSpec(
            num_scalar_prefetch=1,
            grid=(UB // GB,),
            in_specs=slot_specs(wi) + [whole(iq), whole(hw), pl.BlockSpec((rows, q), lambda g, s: (g, 0))],
            out_specs=(
                pl.BlockSpec((pairs, 2 * q, wi), lambda g, s: (0, 0, 0)),
                pl.BlockSpec((pairs, 2 * q), lambda g, s: (0, 0)),
                pl.BlockSpec((rows, wi), lambda g, s: (g, 0)),
            ),
            scratch_shapes=[
                pltpu.VMEM((rows, wi), BF16),
                pltpu.VMEM((wi, rows), BF16),
                pltpu.VMEM((pairs, wi, 2 * q), F32),
                pltpu.VMEM((rows, wi), F32),
            ],
        ),
        out_shape=(
            jax.ShapeDtypeStruct((pairs, 2 * q, wi), BF16),
            jax.ShapeDtypeStruct((pairs, 2 * q), F32),
            jax.ShapeDtypeStruct((UB * BLK, wi), F32),
        ),
        compiler_params=pltpu.CompilerParams(vmem_limit_bytes=VMEM_LIMIT),
        name="backward",
    )(source, *([idx] * GB), iq, hw, grad)


def return_kernel(n_ctx, n_head, pick, dk, out, got_a, part, got_b, slots, landed,
                  ra, rb, rc, sa, sb, sc, sx, sp, so):
    me = lax.axis_index("ctx")
    head, x, core, partner = place()
    n_x = n_head // 2
    per = slots.shape[1]
    others = [lax.rem(me + k, n_ctx) for k in range(1, n_ctx)]
    xs = [lax.rem(x + k, n_x) for k in range(1, n_x)]
    greet([{"ctx": o} for o in others] + [{"head": v * 2 + core} for v in xs] + [{"head": partner}])
    pending = []
    order = xs + [x]
    for v in order:
        c = remote(dk.at[v * 2 + 1 - core], got_a.at[v], sa.at[v], ra.at[v], {"head": partner})
        c.start()
        pending.append(c)
    for i, v in enumerate(order):
        remote(got_a.at[v], got_a.at[v], sa.at[v], ra.at[v], {"head": partner}).wait_recv()
        part[v] = dk[v * 2 + core] + got_a[v]
        if i < n_x - 1:
            c = remote(part.at[v], got_b.at[x], sb.at[v], rb.at[x], {"head": v * 2 + core})
            c.start()
            pending.append(c)
    for v in xs:
        remote(got_b.at[v], got_b.at[v], sb.at[v], rb.at[v], {"head": partner}).wait_recv()
        part[x] += got_b[v]

    for i, o in enumerate(others + [me]):
        def fill(k, carry, o=o):
            slots[o, k] = part[x, pick[o, k]]
            return carry

        lax.fori_loop(0, per, fill, 0)
        if i < n_ctx - 1:
            c = remote(slots.at[o], landed.at[me, head], sc.at[i], rc.at[me, head], {"ctx": o})
            c.start()
            pending.append(c)
    landed[me, head] = slots[me]

    def arrived(o, h):
        remote(landed.at[o, h], landed.at[o, h], sc.at[0], rc.at[o, h], {"head": partner}).wait_recv()

    def send(o, h, sem, to):
        c = remote(landed.at[o, h], landed.at[o, h], sem, rc.at[o, h], {"head": to})
        c.start()
        pending.append(c)

    sources = [me] + [lax.rem(me + n_ctx - k, n_ctx) for k in range(1, n_ctx)]
    for i, o in enumerate(sources):
        if i > 0:
            arrived(o, head)
        for j, v in enumerate(xs):
            send(o, head, sx.at[i, j], v * 2 + core)
        send(o, head, sp.at[i, 0], partner)
    for i, o in enumerate(sources):
        for j, v in enumerate(xs):
            arrived(o, v * 2 + core)
            send(o, v * 2 + core, sp.at[i, 1 + j], partner)
    for i, o in enumerate(sources):
        for v in [x] + xs:
            arrived(o, v * 2 + 1 - core)
    for c in pending:
        c.wait_send()
    c = pltpu.make_async_copy(landed, out, so)
    c.start()
    c.wait()


def give_back(n_ctx, n_head, pick, dk):
    _, u, _, wi = dk.shape
    n_x = n_head // 2
    per = pick.shape[1]
    dma = pltpu.SemaphoreType.DMA
    vm = pl.BlockSpec(memory_space=pltpu.VMEM)
    return pl.pallas_call(
        functools.partial(return_kernel, n_ctx, n_head),
        out_shape=jax.ShapeDtypeStruct((n_ctx, n_head, per, BLK, wi), F32),
        in_specs=[pl.BlockSpec(memory_space=pltpu.SMEM), vm],
        out_specs=pl.BlockSpec(memory_space=pl.ANY),
        scratch_shapes=[
            pltpu.VMEM((n_x, u, BLK, wi), F32),
            pltpu.VMEM((n_x, u, BLK, wi), F32),
            pltpu.VMEM((n_x, u, BLK, wi), F32),
            pltpu.VMEM((n_ctx, per, BLK, wi), F32),
            pltpu.VMEM((n_ctx, n_head, per, BLK, wi), F32),
            dma((n_x,)), dma((n_x,)), dma((n_ctx, n_head)),
            dma((n_x,)), dma((n_x,)), dma((n_ctx,)), dma((n_ctx, n_x)), dma((n_ctx, n_x)),
            dma(()),
        ],
        compiler_params=pltpu.CompilerParams(
            collective_id=2, has_side_effects=True, vmem_limit_bytes=VMEM_LIMIT
        ),
        name="give_back",
    )(pick, dk)


def land_kernel(asked, got, out):
    out[...] = jnp.zeros_like(out)

    def one(f, carry):
        @pl.when(asked[f] >= 0)
        def _():
            out[asked[f]] += got[f]

        return carry

    lax.fori_loop(0, got.shape[0], one, 0)


def land(asked, got, blocks):
    return pl.pallas_call(
        land_kernel,
        out_shape=jax.ShapeDtypeStruct((blocks,) + got.shape[1:], F32),
        in_specs=[pl.BlockSpec(memory_space=pltpu.SMEM), pl.BlockSpec(memory_space=pltpu.VMEM)],
        out_specs=pl.BlockSpec(memory_space=pltpu.VMEM),
        compiler_params=pltpu.CompilerParams(vmem_limit_bytes=VMEM_LIMIT),
        name="land",
    )(asked, got)


def body(
    main_queries,
    latent_keys,
    lse,
    index_queries,
    index_keys,
    head_weights,
    loss_cotangent,
    block_ids,
):
    n_ctx = lax.axis_size("ctx")
    n_head = lax.axis_size("head")
    me = lax.axis_index("ctx")
    head = lax.axis_index("head")
    q, hm, wl = main_queries.shape
    key_rows, wi = index_keys.shape
    ih = index_queries.shape[1]
    owner_blocks = key_rows // BLK
    per = 2 * UB // n_ctx // n_head
    per_head = UB // n_head
    all_blocks = owner_blocks * n_ctx
    n_slot = n_ctx * n_head * per
    blocks = jnp.arange(all_blocks, dtype=jnp.int32)
    present = jnp.any(block_ids.reshape(-1)[:, None] == blocks[None, :], axis=0)
    grid = present.astype(jnp.int32).reshape(n_ctx, owner_blocks)
    count = jnp.sum(grid, axis=1)
    first = jnp.cumsum(count) - count
    inner = jnp.cumsum(grid, axis=1) - 1
    union = (first[:, None] + inner).reshape(-1)
    inner = inner.reshape(-1)
    owner, local = blocks // owner_blocks, blocks % owner_blocks
    klass, turn = union % n_head, inner // n_head
    slot = (owner * n_head + klass) * per + turn
    spot = klass * per_head + union // n_head
    slot_iota = jnp.arange(n_slot, dtype=jnp.int32)
    union_iota = jnp.arange(UB, dtype=jnp.int32)
    in_slot = present[:, None] & (slot[:, None] == slot_iota[None, :])
    in_union = present[:, None] & (spot[:, None] == union_iota[None, :])
    wanted = jnp.max(jnp.where(in_slot, local[:, None], -1), axis=0)
    pick = jnp.max(jnp.where(in_slot, (union // n_head)[:, None], 0), axis=0)
    source = jnp.max(jnp.where(in_union, slot[:, None], 0), axis=0)
    union_block = jnp.max(jnp.where(in_union, blocks[:, None], 0), axis=0)
    asked = lax.all_to_all(
        wanted.reshape(n_ctx, n_head * per), "ctx", split_axis=0, concat_axis=0, tiled=True
    )
    lat_local = latent_keys.reshape(owner_blocks, BLK, wl)
    idx_local = index_keys.reshape(owner_blocks, BLK, wi)
    want3 = wanted.reshape(n_ctx, n_head, per)
    ask3 = asked.reshape(n_ctx, n_head, per)
    mine = jnp.maximum(lax.dynamic_index_in_dim(ask3, head, 1, keepdims=False), 0)
    own = jnp.maximum(lax.dynamic_index_in_dim(want3, me, 0, keepdims=False), 0)
    my_pick = lax.dynamic_index_in_dim(pick.reshape(n_ctx, n_head, per), head, 1, keepdims=False)
    lat_got, idx_got = fetch(
        n_ctx, n_head, lat_local[mine], idx_local[mine], lat_local[own], idx_local[own]
    )
    lat_got = lat_got.reshape(n_slot, BLK, wl)
    idx_got = idx_got.reshape(n_slot, BLK, wi)
    chosen = jnp.any(union_block[:, None, None] == block_ids[None, :, :], axis=2)
    query_pos = all_blocks * BLK - q * n_ctx + me * q + jnp.arange(q, dtype=jnp.int32)
    lim = jnp.where(chosen, query_pos[None, :] - union_block[:, None] * BLK, -1)
    mq = main_queries.transpose(1, 0, 2).reshape(hm // 2, 2 * q, wl)
    iq = index_queries.transpose(1, 0, 2).reshape(ih // 2, 2 * q, wi)
    lse2 = (lse * LOG2E).T.reshape(hm // 2, 2 * q)
    hw2 = head_weights.T.reshape(ih // 2, 2 * q)
    mass, score = forward(source, lat_got, idx_got, mq, lse2, iq, hw2, lim)
    grad = score_grads(n_head, mass, score, loss_cotangent.reshape(1, q))
    dq, dw, dk = backward(source, idx_got, iq, hw2, grad)
    d_queries = dq.reshape(ih, q, wi).transpose(1, 0, 2)
    d_weights = dw.reshape(ih, q).T
    back = give_back(n_ctx, n_head, my_pick, dk.reshape(n_head, per_head, BLK, wi))
    d_keys = land(asked.reshape(-1), back.reshape(n_slot, BLK, wi), owner_blocks)
    return (d_queries, d_weights, d_keys.reshape(key_rows, wi))


def solution(mesh):
    placed = (
        P(("grp", "ctx"), "head", None),
        P(("grp", "ctx"), None),
        P(("grp", "ctx"), "head"),
        P(("grp", "ctx"), "head", None),
        P(("grp", "ctx"), None),
        P(("grp", "ctx"), "head"),
        P(("grp", "ctx")),
        P(("grp", "ctx"), None),
    )
    return jax.shard_map(
        body,
        mesh=mesh,
        in_specs=placed,
        out_specs=(
            P(("grp", "ctx"), "head", None),
            P(("grp", "ctx"), "head"),
            P(("grp", "ctx"), None),
        ),
        check_vma=False,
    )
```

time: 704 us -> 384 us (0.55)
  waiting for transfers between devices: 435 us -> 0.01 us
  Pallas kernels: 0 us -> 330 us
  matrix products: 108 us -> 0 us
  other arithmetic: 54.8 us -> 5.62 us
  local copies, waits for them, and re-layouts: 62.9 us -> 37.5 us
  between operations: 14.3 us -> 0.72 us
  blocking collectives: 11.7 us -> 0 us
  starting transfers between devices: 15.1 us -> 6.32 us
    pallas_call x0 -> x6, Pallas kernels: none -> 330 us  [the longest x1 101 us: fetch(): pl.pallas_call(functools.partial(fetch_kernel, n_ctx, n_head), out_shape=...]
    all_to_all x3 -> x1, waiting for transfers between devices: 314 us -> 0.01 us  [body(): lax.all_to_all(wanted.reshape(n_ctx, n_head * per), 'ctx', split_axis=0,...]
    psum x2 -> x0, waiting for transfers between devices: 121 us -> none  [the longest x1 84.7 us: body(): mass_whole, score_whole = lax.psum((mass_part, score_part), 'head')]
    dot_general x13 -> x0, matrix products: 108 us -> none  [the longest x8 55.8 us: head_mass(): jnp.einsum('qhc,sc->qhs', main_queries, group_keys, preferred_element_typ...]
    another operation x3 -> x2, other arithmetic: 29.2 us -> 0.42 us  [the longest x1 0.24 us: body(): inner = jnp.cumsum(grid, axis=1) - 1]
    dot_general x1 -> x0, other arithmetic: 13.5 us -> none  [body(): jnp.einsum('qs,qjs->qj', score_grad, activated, precision=lax.Precision.H...]
    all_to_all x1 -> x0, blocking collectives: 11.7 us -> none  [body(): lax.all_to_all(wanted, 'ctx', split_axis=0, concat_axis=0, tiled=True)]
    gather x5 -> x4, local copies, waits for them, and re-layouts: 21.1 us -> 12.5 us  [the longest x1 4.88 us: body(): lat_local[own]]
  transfers between devices with their start and end apart: 5 -> 1, of which waited for: 5 -> 0; matrix products, arithmetic and copies ran while one was open for 10% -> 7% of each run, Pallas kernels for 0% -> 0%
where the time goes in v1:
time: 384 us; the launch traced here: 380 us
  Pallas kernels  330 us (86%)
  local copies, waits for them, and re-layouts  37.5 us (10%)
  starting transfers between devices  6.32 us (2%)
  other arithmetic  5.62 us (1%)
    pallas_call x1, Pallas kernels, fetch(): pl.pallas_call(functools.partial(fetch_kernel, n_ctx, n_head), out_shape=...  101 us
    pallas_call x1, Pallas kernels, forward(): pl.pallas_call(forward_kernel, grid_spec=pltpu.PrefetchScalarGridSpec(num...  75.7 us
    pallas_call x1, Pallas kernels, give_back(): pl.pallas_call(functools.partial(return_kernel, n_ctx, n_head), out_shape...  56.9 us
    pallas_call x1, Pallas kernels, score_grads(): pl.pallas_call(functools.partial(grad_kernel, n_head), out_shape=jax.Shap...  49.1 us
    pallas_call x1, Pallas kernels, backward(): pl.pallas_call(backward_kernel, grid_spec=pltpu.PrefetchScalarGridSpec(nu...  42 us
    unnamed x10, local copies, waits for them, and re-layouts  8.58 us
  transfers between devices with their start and end apart: 1, of which 0 were waited for; matrix products, arithmetic and copies ran while one was open for 7% of the time, Pallas kernels for 0%

profile of v1, /device:TPU:0, one launch (start us, length us, event | category | flops | bytes accessed | tf_op | source)
XLA Modules:
  0.0 380.4 jit_solution(17544457752467349112)
XLA Ops:
  0.6 0.0 copy-start
  0.6 0.9 copy.28
  1.5 0.1 eq.29
  1.6 1.9 fusion
  3.5 0.1 reshape.251
  3.6 0.1 reduce_sum.9
  3.7 0.2 reduce_window_sum.18
  4.0 0.2 reduce-window.8
  4.1 0.1 add.119
  4.2 0.1 add.120
  4.3 0.1 sub.44
  4.4 0.2 select_reduce_fusion
  4.6 0.7 all_to_all.6
  5.3 6.3 %all-to-all-start = ((s32[4,1,32]{2,1,0:T(1,128)}), s32[4,1,32]{2,1,0:T(1,128)S(1)}, u32[]{:S(2)}, u32[]{:S(2)}) async-start(s32[4,1,32]{2,1,0:T(1,128)} %bitcast.3), calls=%async_computation | async-start | bytes 4096 | tf_op jit(solution)/shard_map/all_to_all | solution.py:522
  11.6 0.1 reshape.236
  11.7 0.6 select_reduce_fusion.2
  12.3 0.9 compare_reduce_fusion
  13.3 0.1 reshape.270
  13.4 0.0 copy-start.2
  13.4 7.7 %copy.29 = bf16[4096,576]{1,0:T(8,128)(2,1)} copy(bf16[4096,576]{0,1:T(8,128)(2,1)} %param.9) | data formatting | bytes 9437184 | tf_op args[1]
  21.0 0.0 copy-done.2
  21.1 0.1 reshape.247
  21.1 0.6 constant_dynamic-slice_fusion
  21.8 0.7 subtract_select_fusion.refs_20_
  22.4 0.0 copy-start.1
  22.4 0.0 copy-start.3
  22.4 4.9 %gather_fusion.2 = bf16[32,64,576]{2,1,0:T(8,128)(2,1)} fusion(bf16[64,64,576]{2,1,0:T(8,128)(2,1)} %bitcast.57, s32[1024]{0:T(1024)S(1)} %pad_clamp_fusion), kind=kCustom, calls=%fused_computation.2 | custom fusion | bytes 4718720 | tf_op jit(solution)/shard_map/gather | solution.py:533
  27.3 0.0 copy-done
  27.3 1.4 gather_fusion.3
  28.7 0.0 copy-done.1
  28.7 0.9 copy.31
  29.7 0.0 copy-done.3
  29.7 0.6 reshape.239.refs_19_.refs_9_
  30.3 7.6 %copy.32 = bf16[32,128,576]{2,1,0:T(8,128)(2,1)} copy(bf16[32,128,576]{1,2,0:T(8,128)(2,1)} %bitcast.64) | data formatting | bytes 9437184 | tf_op jit(solution)/shard_map/transpose | solution.py:540
  37.9 0.6 reshape.242.refs_17_
  38.5 0.0 all-to-all-done
  38.5 0.5 broadcast.296
  39.0 0.7 reduce.9
  39.7 0.1 reshape.234
  39.8 0.1 reshape.254
  39.9 4.8 %gather_fusion = bf16[32,64,576]{2,1,0:T(8,128)(2,1)} fusion(bf16[64,64,576]{2,1,0:T(8,128)(2,1)} %bitcast.58, s32[1024]{0:T(1024)S(1)} %pad_clamp_fusion.1), kind=kCustom, calls=%fused_computation | custom fusion | bytes 4718720 | tf_op jit(solution)/shard_map/gather | solution.py:533
  44.7 1.4 gather_fusion.1
  46.1 100.9 %fetch.1 = (bf16[4,4,8,64,576]{4,3,2,1,0:T(8,128)(2,1)}, bf16[4,4,8,64,128]{4,3,2,1,0:T(8,128)(2,1)}) custom-call(bf16[4,8,64,576]{3,2,1,0:T(8,128)(2,1)} %bitcast.61, bf16[4,8,64,128]{3,2,1,0:T(8,128)(2,1)} %bitcast.67, bf16[4,8,64,576]{3,2,1,0:T(8,128)(2,1)} %bitcast.60, bf16[4,8,64,128]{3,2,1,0:T(8,128)(2,1)} %bitcast.66), custom_call_target="tpu_custom_call" | custom-call | tf_op jit(solution)/shard_map/fetch/pallas_call | solution.py:104
  147.0 75.7 %forward.1 = (f32[4096,128]{1,0:T(8,128)}, f32[4096,128]{1,0:T(8,128)}) custom-call(s32[64]{0:T(128)} %get-tuple-element.20.src, bf16[128,64,576]{2,1,0:T(8,128)(2,1)} %bitcast.32, bf16[128,64,576]{2,1,0:T(8,128)(2,1)} %bitcast.33, bf16[128,64,576]{2,1,0:T(8,128)(2,1)} %bitcast.34, bf16[128,64,576]{2,1,0:T(8,128)(2,1)} %bitcast.35, ...), custom_call_target="tpu_custom_call" | custom-call | tf_op jit(solution)/shard_map/forward/pallas_call | solution.py:172
  222.6 49.1 %score_grads.1.refs_10_ = f32[4096,128]{1,0:T(8,128)} custom-call(f32[4096,128]{1,0:T(8,128)} %get-tuple-element.12.mass, f32[4096,128]{1,0:T(8,128)} %get-tuple-element.13.score, f32[1,128]{1,0:T(1,128)} %bitcast.76), custom_call_target="tpu_custom_call" | custom-call | tf_op jit(solution)/shard_map/score_grads/pallas_call | solution.py:272
  271.7 42.0 %backward.1 = (bf16[8,256,128]{2,1,0:T(8,128)(2,1)}, f32[8,256]{1,0:T(8,128)}, f32[4096,128]{1,0:T(8,128)}) custom-call(s32[64]{0:T(128)} %get-tuple-element.20.src, bf16[128,64,128]{2,1,0:T(8,128)(2,1)} %bitcast.48, bf16[128,64,128]{2,1,0:T(8,128)(2,1)} %bitcast.49, bf16[128,64,128]{2,1,0:T(8,128)(2,1)} %bitcast.50, bf16[128,64,128]{2,1,0:T(8,128)(2,1)} %bitcast.51, ...), custom_call_target="tpu_custom_call" | custom-call | tf_op jit(solution)/shard_map/backward/pallas_call | solution.py:333
  313.7 0.6 reshape.246.asked
  314.3 2.2 copy.35
  316.5 1.3 reshape.245
  317.8 56.9 %give_back.1 = f32[4,4,8,64,128]{4,3,2,1,0:T(8,128)} custom-call(s32[4,8]{1,0:T(4,128)} %bitcast.73, f32[4,16,64,128]{3,2,1,0:T(8,128)} %bitcast.68), custom_call_target="tpu_custom_call" | custom-call | tf_op jit(solution)/shard_map/give_back/pallas_call | solution.py:434
  374.8 5.7 %land.1 = f32[64,64,128]{2,1,0:T(8,128)} custom-call(s32[128]{0:T(128)} %reshape.246.asked, f32[128,64,128]{2,1,0:T(8,128)} %bitcast.59), custom_call_target="tpu_custom_call" | custom-call | tf_op jit(solution)/shard_map/land/pallas_call | solution.py:470
  (11 shorter events, 0.1 us)
Async XLA Ops:
  0.6 26.7 %copy-start = (bf16[4096,128]{1,0:T(8,128)(2,1)S(1)}, bf16[4096,128]{1,0:T(8,128)(2,1)}, u32[]{:S(2)}) copy-start(bf16[4096,128]{1,0:T(8,128)(2,1)} %param.12) | copy-start | bytes 3145732
  5.3 33.2 %all-to-all-start = ((s32[4,1,32]{2,1,0:T(1,128)}), s32[4,1,32]{2,1,0:T(1,128)S(1)}, u32[]{:S(2)}, u32[]{:S(2)}) async-start(s32[4,1,32]{2,1,0:T(1,128)} %bitcast.3), calls=%async_computation | async-start | bytes 4096 | tf_op jit(solution)/shard_map/all_to_all | solution.py:522
  13.4 7.7 %copy-start.2 = (f32[128,32]{0,1:T(8,128)S(1)}, f32[128,32]{0,1:T(8,128)}, u32[]{:S(2)}) copy-start(f32[128,32]{0,1:T(8,128)} %param.10) | copy-start | bytes 49156
  22.4 6.3 %copy-start.1 = (bf16[128,16,128]{2,1,0:T(8,128)(2,1)S(1)}, bf16[128,16,128]{2,1,0:T(8,128)(2,1)}, u32[]{:S(2)}) copy-start(bf16[128,16,128]{2,1,0:T(8,128)(2,1)} %param.11) | copy-start | bytes 1572868
  22.4 7.2 %copy-start.3 = (f32[128,16]{0,1:T(8,128)S(1)}, f32[128,16]{0,1:T(8,128)}, u32[]{:S(2)}) copy-start(f32[128,16]{0,1:T(8,128)} %param.13) | copy-start | bytes 24580

commit v2 on v1

--- a/solution.py
+++ b/solution.py
@@ -39,54 +39,66 @@
     )
 
 
-def fetch_kernel(n_ctx, n_head, lat_mine, idx_mine, lat_own, idx_own, lat_got, idx_got,
+def fetch_kernel(n_ctx, n_head, cuts, lat_mine, idx_mine, lat_own, idx_own, lat_got, idx_got,
                  own_sem, recv_sem, s_ctx, s_x, s_core):
     me = lax.axis_index("ctx")
     head, x, core, partner = place()
     n_x = n_head // 2
+    piece = lat_mine.shape[1] // cuts
     others = [lax.rem(me + k, n_ctx) for k in range(1, n_ctx)]
+    sources = [lax.rem(me + n_ctx - k, n_ctx) for k in range(1, n_ctx)]
     xs = [lax.rem(x + k, n_x) for k in range(1, n_x)]
     greet([{"ctx": o} for o in others] + [{"head": v * 2 + core} for v in xs] + [{"head": partner}])
-    mine, own, got = (idx_mine, lat_mine), (idx_own, lat_own), (idx_got, lat_got)
+    units = range(cuts + 1)
+
+    def mine(a, o):
+        return idx_mine.at[o] if a == 0 else lat_mine.at[o, pl.ds((a - 1) * piece, piece)]
+
+    def got(a, o, h):
+        return idx_got.at[o, h] if a == 0 else lat_got.at[o, h, pl.ds((a - 1) * piece, piece)]
+
     pending = []
-    for a in range(2):
+    for a in units:
         for i, o in enumerate(others):
-            c = remote(mine[a].at[o], got[a].at[me, head], s_ctx.at[a, i],
+            c = remote(mine(a, o), got(a, me, head), s_ctx.at[a, i],
                        recv_sem.at[a, me, head], {"ctx": o})
             c.start()
             pending.append(c)
-    locals_ = []
-    for a in range(2):
-        c = pltpu.make_async_copy(own[a], got[a].at[me], own_sem.at[a])
+    locals_ = [
+        pltpu.make_async_copy(idx_own, idx_got.at[me], own_sem.at[0]),
+        pltpu.make_async_copy(lat_own, lat_got.at[me], own_sem.at[1]),
+    ]
+    for c in locals_:
         c.start()
-        locals_.append(c)
 
     def arrived(a, o, h):
-        remote(got[a].at[o, h], got[a].at[o, h], s_core.at[a, 0, 0], recv_sem.at[a, o, h],
+        remote(got(a, o, h), got(a, o, h), s_core.at[a, 0, 0], recv_sem.at[a, o, h],
                {"head": partner}).wait_recv()
 
-    def forward(a, i, o, h, slot):
-        c = remote(got[a].at[o, h], got[a].at[o, h], s_core.at[a, i, slot],
-                   recv_sem.at[a, o, h], {"head": partner})
+    def send(a, o, h, sem, to):
+        c = remote(got(a, o, h), got(a, o, h), sem, recv_sem.at[a, o, h], {"head": to})
         c.start()
         pending.append(c)
 
-    sources = [lax.rem(me + n_ctx - k, n_ctx) for k in range(1, n_ctx)]
-    for a in range(2):
+    def across(a):
         for i, o in enumerate(sources):
             arrived(a, o, head)
             for j, v in enumerate(xs):
-                c = remote(got[a].at[o, head], got[a].at[o, head], s_x.at[a, i, j],
-                           recv_sem.at[a, o, head], {"head": v * 2 + core})
-                c.start()
-                pending.append(c)
-            forward(a, i, o, head, 0)
-    for a in range(2):
+                send(a, o, head, s_x.at[a, i, j], v * 2 + core)
+            send(a, o, head, s_core.at[a, i, 0], partner)
+
+    def along(a):
         for i, o in enumerate(sources):
             for j, v in enumerate(xs):
                 arrived(a, o, v * 2 + core)
-                forward(a, i, o, v * 2 + core, 1 + j)
-    for a in range(2):
+                send(a, o, v * 2 + core, s_core.at[a, i, 1 + j], partner)
+
+    for a in units:
+        across(a)
+        if a > 0:
+            along(a - 1)
+    along(cuts)
+    for a in units:
         for i, o in enumerate(sources):
             for v in [x] + xs:
                 arrived(a, o, v * 2 + 1 - core)
@@ -100,9 +112,10 @@
     per, _, wl = lat_mine.shape[1:]
     wi = idx_mine.shape[-1]
     n_x = n_head // 2
+    cuts = math.gcd(per, 4)
     dma = pltpu.SemaphoreType.DMA
     return pl.pallas_call(
-        functools.partial(fetch_kernel, n_ctx, n_head),
+        functools.partial(fetch_kernel, n_ctx, n_head, cuts),
         out_shape=(
             jax.ShapeDtypeStruct((n_ctx, n_head, per, BLK, wl), BF16),
             jax.ShapeDtypeStruct((n_ctx, n_head, per, BLK, wi), BF16),
@@ -111,18 +124,47 @@
         out_specs=(pl.BlockSpec(memory_space=pl.ANY),) * 2,
         scratch_shapes=[
             dma((2,)),
-            dma((2, n_ctx, n_head)),
-            dma((2, n_ctx)),
-            dma((2, n_ctx, n_x)),
-            dma((2, n_ctx, n_x)),
+            dma((cuts + 1, n_ctx, n_head)),
+            dma((cuts + 1, n_ctx)),
+            dma((cuts + 1, n_ctx, n_x)),
+            dma((cuts + 1, n_ctx, n_x)),
         ],
         compiler_params=pltpu.CompilerParams(collective_id=0, has_side_effects=True),
         name="fetch",
     )(lat_mine, idx_mine, lat_own, idx_own)
 
 
-def nt(a, b):
-    return lax.dot_general(a, b, (((1,), (1,)), ((), ())), preferred_element_type=F32)
+def select_kernel(mine, own, lat, idx, lat_mine, idx_mine, lat_own, idx_own, sem):
+    def one(k, carry):
+        pltpu.make_async_copy(lat.at[mine[k]], lat_mine.at[k], sem.at[0]).start()
+        pltpu.make_async_copy(idx.at[mine[k]], idx_mine.at[k], sem.at[1]).start()
+        return carry
+
+    def two(k, carry):
+        pltpu.make_async_copy(lat.at[own[k]], lat_own.at[k], sem.at[2]).start()
+        pltpu.make_async_copy(idx.at[own[k]], idx_own.at[k], sem.at[3]).start()
+        return carry
+
+    lax.fori_loop(0, mine.shape[0], one, 0)
+    lax.fori_loop(0, own.shape[0], two, 0)
+    for i, r in enumerate((lat_mine, idx_mine, lat_own, idx_own)):
+        pltpu.make_async_copy(r, r, sem.at[i]).wait()
+
+
+def select(mine, own, lat, idx):
+    shapes = tuple(
+        jax.ShapeDtypeStruct((n,) + a.shape[1:], BF16)
+        for n in (mine.shape[0], own.shape[0]) for a in (lat, idx)
+    )
+    anywhere = pl.BlockSpec(memory_space=pl.ANY)
+    return pl.pallas_call(
+        select_kernel,
+        out_shape=shapes,
+        in_specs=[pl.BlockSpec(memory_space=pltpu.SMEM)] * 2 + [anywhere] * 2,
+        out_specs=(anywhere,) * 4,
+        scratch_shapes=[pltpu.SemaphoreType.DMA((4,))],
+        name="select",
+    )(mine, own, lat, idx)
 
 
 def forward_kernel(src, *refs):
@@ -137,19 +179,20 @@
     score[...] = jnp.zeros_like(score)
 
     def main(i, carry):
-        s = nt(keys[...], mq[i])
+        both = jnp.concatenate([mq[2 * i], mq[2 * i + 1]], axis=1)
+        s = jnp.dot(keys[...], both, preferred_element_type=F32)
         e = jnp.exp2(s * (ATTN_SCALE * LOG2E) - lse[pl.ds(i, 1), :])
         mass[...] += e[:, :q] + e[:, q:]
         return carry
 
-    lax.fori_loop(0, mq.shape[0], main, 0)
+    lax.fori_loop(0, mq.shape[0] // 2, main, 0, unroll=True)
 
     def side(i, carry):
-        v = jnp.maximum(nt(ikeys[...], iq[i]), 0.0) * hw[pl.ds(i, 1), :]
+        v = jnp.maximum(jnp.dot(ikeys[...], iq[i], preferred_element_type=F32), 0.0) * hw[pl.ds(i, 1), :]
         score[...] += v[:, :q] + v[:, q:]
         return carry
 
-    lax.fori_loop(0, iq.shape[0], side, 0)
+    lax.fori_loop(0, iq.shape[0], side, 0, unroll=True)
     offset = lax.broadcasted_iota(jnp.int32, (BLK, q), 0)
     for b in range(GB):
         rows = slice(b * BLK, (b + 1) * BLK)
@@ -185,7 +228,7 @@
     )(source, *([lat] * GB), *([idx] * GB), mq, lse, iq, hw, lim)
 
 
-def grad_kernel(n_head, mass, score, cot, grad, got_a, part, got_b, stat, whole,
+def grad_kernel(n_head, mass, score, cot, grad, got_a, part, half, got_s, got_m, stat, whole,
                 ra, rb, rs, rg, sa, sb, ss, sg):
     head, x, core, partner = place()
     n_x = n_head // 2
@@ -195,6 +238,7 @@
     greet([{"head": h} for h in heads])
     rows = lambda h: pl.ds(pl.multiple_of(h * span, span), span)
     both = (score, mass)
+    got_b = (got_s, got_m)
     pending = []
     order = xs + [x]
     for v in order:
@@ -209,15 +253,17 @@
                    {"head": partner}).wait_recv()
             part[a, v] = both[a][rows(v * 2 + core), :] + got_a[a, v]
             if i < n_x - 1:
-                c = remote(part.at[a, v], got_b.at[a, x], sb.at[a, v], rb.at[a, x],
+                if a == 1:
+                    half[v] = part[1, v].astype(BF16)
+                c = remote((part.at[0, v] if a == 0 else half.at[v]), got_b[a].at[x], sb.at[a, v], rb.at[a, x],
                            {"head": v * 2 + core})
                 c.start()
                 pending.append(c)
     for v in xs:
         for a in range(2):
-            remote(got_b.at[a, v], got_b.at[a, v], sb.at[a, v], rb.at[a, v],
+            remote(got_b[a].at[v], got_b[a].at[v], sb.at[a, v], rb.at[a, v],
                    {"head": partner}).wait_recv()
-            part[a, x] += got_b[a, v]
+            part[a, x] += got_b[a][v].astype(F32)
     top = jnp.max(part[0, x], axis=0, keepdims=True)
     expo = jnp.exp(part[0, x] - top)
     stat[head, 0:1, :] = top
@@ -240,7 +286,7 @@
         mass_total += stat[h, 2:3, :]
     left = cot[...] * jnp.exp(top - best) / total
     right = cot[...] / mass_total
-    whole[head] = expo * left - part[1, x] * right
+    whole[head] = (expo * left - part[1, x] * right).astype(BF16)
 
     def send(h, sem, to):
         c = remote(whole.at[h], whole.at[h], sem, rg.at[h], {"head": to})
@@ -271,15 +317,17 @@
     vm = pl.BlockSpec(memory_space=pltpu.VMEM)
     return pl.pallas_call(
         functools.partial(grad_kernel, n_head),
-        out_shape=jax.ShapeDtypeStruct((keys, q), F32),
+        out_shape=jax.ShapeDtypeStruct((keys, q), BF16),
         in_specs=[vm] * 3,
         out_specs=vm,
         scratch_shapes=[
             pltpu.VMEM((2, n_x, span, q), F32),
             pltpu.VMEM((2, n_x, span, q), F32),
-            pltpu.VMEM((2, n_x, span, q), F32),
+            pltpu.VMEM((n_x, span, q), BF16),
+            pltpu.VMEM((n_x, span, q), F32),
+            pltpu.VMEM((n_x, span, q), BF16),
             pltpu.VMEM((n_head, 8, q), F32),
-            pltpu.VMEM((n_head, span, q), F32),
+            pltpu.VMEM((n_head, span, q), BF16),
             dma((2, n_x)), dma((2, n_x)), dma((n_head,)), dma((n_head,)),
             dma((2, n_x)), dma((2, n_x)), dma((n_head,)), dma((n_head + 1,)),
         ],
@@ -292,7 +340,7 @@
 
 def backward_kernel(src, *refs):
     idx = refs[:GB]
-    iq, hw, grad, dq, dw, dk, ikeys, tkeys, acc, gacc = refs[GB:]
+    iq, iqt, hw, grad, dq, dw, dk, ikeys, tkeys, acc, gacc = refs[GB:]
     q = grad.shape[1]
     step = pl.program_id(0)
 
@@ -307,15 +355,16 @@
     gacc[...] = jnp.zeros_like(gacc)
 
     def one(i, carry):
-        pre = nt(ikeys[...], iq[i])
-        g = jnp.concatenate([grad[...], grad[...]], axis=1)
+        pre = jnp.dot(ikeys[...], iqt[i], preferred_element_type=F32)
+        half = grad[...].astype(F32)
+        g = jnp.concatenate([half, half], axis=1)
         dw[pl.ds(i, 1), :] += jnp.sum(g * jnp.maximum(pre, 0.0), axis=0, keepdims=True)
         pg = jnp.where(pre > 0.0, g * hw[pl.ds(i, 1), :], 0.0).astype(BF16)
         acc[i] += jnp.dot(tkeys[...], pg, preferred_element_type=F32)
         gacc[...] += jnp.dot(pg, iq[i], preferred_element_type=F32)
         return carry
 
-    lax.fori_loop(0, iq.shape[0], one, 0)
+    lax.fori_loop(0, iq.shape[0], one, 0, unroll=True)
     dk[...] = gacc[...]
 
     @pl.when(step == pl.num_programs(0) - 1)
@@ -324,7 +373,7 @@
             dq[i] = jnp.swapaxes(acc[i], 0, 1).astype(BF16)
 
 
-def backward(source, idx, iq, hw, grad):
+def backward(source, idx, iq, iqt, hw, grad):
     q = grad.shape[1]
     wi = idx.shape[-1]
     rows = GB * BLK
@@ -335,7 +384,7 @@
         grid_spec=pltpu.PrefetchScalarGridSpec(
             num_scalar_prefetch=1,
             grid=(UB // GB,),
-            in_specs=slot_specs(wi) + [whole(iq), whole(hw), pl.BlockSpec((rows, q), lambda g, s: (g, 0))],
+            in_specs=slot_specs(wi) + [whole(iq), whole(iqt), whole(hw), pl.BlockSpec((rows, q), lambda g, s: (g, 0))],
             out_specs=(
                 pl.BlockSpec((pairs, 2 * q, wi), lambda g, s: (0, 0, 0)),
                 pl.BlockSpec((pairs, 2 * q), lambda g, s: (0, 0)),
@@ -355,10 +404,10 @@
         ),
         compiler_params=pltpu.CompilerParams(vmem_limit_bytes=VMEM_LIMIT),
         name="backward",
-    )(source, *([idx] * GB), iq, hw, grad)
-
-
-def return_kernel(n_ctx, n_head, pick, dk, out, got_a, part, got_b, slots, landed,
+    )(source, *([idx] * GB), iq, iqt, hw, grad)
+
+
+def return_kernel(n_ctx, n_head, pick, dk, out, got_a, part, half, got_b, slots, landed,
                   ra, rb, rc, sa, sb, sc, sx, sp, so):
     me = lax.axis_index("ctx")
     head, x, core, partner = place()
@@ -377,16 +426,17 @@
         remote(got_a.at[v], got_a.at[v], sa.at[v], ra.at[v], {"head": partner}).wait_recv()
         part[v] = dk[v * 2 + core] + got_a[v]
         if i < n_x - 1:
-            c = remote(part.at[v], got_b.at[x], sb.at[v], rb.at[x], {"head": v * 2 + core})
+            half[v] = part[v].astype(BF16)
+            c = remote(half.at[v], got_b.at[x], sb.at[v], rb.at[x], {"head": v * 2 + core})
             c.start()
             pending.append(c)
     for v in xs:
         remote(got_b.at[v], got_b.at[v], sb.at[v], rb.at[v], {"head": partner}).wait_recv()
-        part[x] += got_b[v]
+        part[x] += got_b[v].astype(F32)
 
     for i, o in enumerate(others + [me]):
         def fill(k, carry, o=o):
-            slots[o, k] = part[x, pick[o, k]]
+            slots[o, k] = part[x, pick[o, k]].astype(BF16)
             return carry
 
         lax.fori_loop(0, per, fill, 0)
@@ -433,15 +483,16 @@
     vm = pl.BlockSpec(memory_space=pltpu.VMEM)
     return pl.pallas_call(
         functools.partial(return_kernel, n_ctx, n_head),
-        out_shape=jax.ShapeDtypeStruct((n_ctx, n_head, per, BLK, wi), F32),
+        out_shape=jax.ShapeDtypeStruct((n_ctx, n_head, per, BLK, wi), BF16),
         in_specs=[pl.BlockSpec(memory_space=pltpu.SMEM), vm],
         out_specs=pl.BlockSpec(memory_space=pl.ANY),
         scratch_shapes=[
             pltpu.VMEM((n_x, u, BLK, wi), F32),
             pltpu.VMEM((n_x, u, BLK, wi), F32),
-            pltpu.VMEM((n_x, u, BLK, wi), F32),
-            pltpu.VMEM((n_ctx, per, BLK, wi), F32),
-            pltpu.VMEM((n_ctx, n_head, per, BLK, wi), F32),
+            pltpu.VMEM((n_x, u, BLK, wi), BF16),
+            pltpu.VMEM((n_x, u, BLK, wi), BF16),
+            pltpu.VMEM((n_ctx, per, BLK, wi), BF16),
+            pltpu.VMEM((n_ctx, n_head, per, BLK, wi), BF16),
             dma((n_x,)), dma((n_x,)), dma((n_ctx, n_head)),
             dma((n_x,)), dma((n_x,)), dma((n_ctx,)), dma((n_ctx, n_x)), dma((n_ctx, n_x)),
             dma(()),
@@ -459,7 +510,7 @@
     def one(f, carry):
         @pl.when(asked[f] >= 0)
         def _():
-            out[asked[f]] += got[f]
+            out[asked[f]] += got[f].astype(F32)
 
         return carry
 
@@ -529,21 +580,30 @@
     mine = jnp.maximum(lax.dynamic_index_in_dim(ask3, head, 1, keepdims=False), 0)
     own = jnp.maximum(lax.dynamic_index_in_dim(want3, me, 0, keepdims=False), 0)
     my_pick = lax.dynamic_index_in_dim(pick.reshape(n_ctx, n_head, per), head, 1, keepdims=False)
+    lat_mine, idx_mine, lat_own, idx_own = select(
+        mine.reshape(-1), own.reshape(-1), lat_local, idx_local
+    )
     lat_got, idx_got = fetch(
-        n_ctx, n_head, lat_local[mine], idx_local[mine], lat_local[own], idx_local[own]
+        n_ctx,
+        n_head,
+        lat_mine.reshape(n_ctx, per, BLK, wl),
+        idx_mine.reshape(n_ctx, per, BLK, wi),
+        lat_own.reshape(n_head, per, BLK, wl),
+        idx_own.reshape(n_head, per, BLK, wi),
     )
     lat_got = lat_got.reshape(n_slot, BLK, wl)
     idx_got = idx_got.reshape(n_slot, BLK, wi)
     chosen = jnp.any(union_block[:, None, None] == block_ids[None, :, :], axis=2)
     query_pos = all_blocks * BLK - q * n_ctx + me * q + jnp.arange(q, dtype=jnp.int32)
     lim = jnp.where(chosen, query_pos[None, :] - union_block[:, None] * BLK, -1)
-    mq = main_queries.transpose(1, 0, 2).reshape(hm // 2, 2 * q, wl)
+    mq = main_queries.transpose(1, 2, 0)
     iq = index_queries.transpose(1, 0, 2).reshape(ih // 2, 2 * q, wi)
+    iqt = iq.transpose(0, 2, 1)
     lse2 = (lse * LOG2E).T.reshape(hm // 2, 2 * q)
     hw2 = head_weights.T.reshape(ih // 2, 2 * q)
-    mass, score = forward(source, lat_got, idx_got, mq, lse2, iq, hw2, lim)
+    mass, score = forward(source, lat_got, idx_got, mq, lse2, iqt, hw2, lim)
     grad = score_grads(n_head, mass, score, loss_cotangent.reshape(1, q))
-    dq, dw, dk = backward(source, idx_got, iq, hw2, grad)
+    dq, dw, dk = backward(source, idx_got, iq, iqt, hw2, grad)
     d_queries = dq.reshape(ih, q, wi).transpose(1, 0, 2)
     d_weights = dw.reshape(ih, q).T
     back = give_back(n_ctx, n_head, my_pick, dk.reshape(n_head, per_head, BLK, wi))

time: 384 us -> 462 us (1.20)
  Pallas kernels: 330 us -> 429 us
  local copies, waits for them, and re-layouts: 37.5 us -> 18.7 us
    pallas_call x1 -> x2, Pallas kernels: 101 us -> 294 us  [the longest x1 192 us: select(): pl.pallas_call(select_kernel, out_shape=shapes, in_specs=[pl.BlockSpec(me...]
    pallas_call x1, Pallas kernels: 75.7 us -> 38.6 us  [forward(): pl.pallas_call(forward_kernel, grid_spec=pltpu.PrefetchScalarGridSpec(num...]
    pallas_call x1, Pallas kernels: 56.9 us -> 33 us  [give_back(): pl.pallas_call(functools.partial(return_kernel, n_ctx, n_head), out_shape...]
    pallas_call x1, Pallas kernels: 42 us -> 21.2 us  [backward(): pl.pallas_call(backward_kernel, grid_spec=pltpu.PrefetchScalarGridSpec(nu...]
    gather x4 -> x0, local copies, waits for them, and re-layouts: 12.5 us -> none  [the longest x1 4.88 us: body(): lat_local[own]]
    pallas_call x1, Pallas kernels: 49.1 us -> 37.1 us  [score_grads(): pl.pallas_call(functools.partial(grad_kernel, n_head), out_shape=jax.Shap...]
    transpose x2 -> x0, local copies, waits for them, and re-layouts: 8.57 us -> none  [the longest x1 7.62 us: body(): mq = main_queries.transpose(1, 0, 2).reshape(hm // 2, 2 * q, wl)]
  transfers between devices with their start and end apart: 1 -> 1, of which waited for: 0 -> 0; matrix products, arithmetic and copies ran while one was open for 7% -> 3% of each run, Pallas kernels for 0% -> 0%
where the time goes in v2:
time: 462 us; the launch traced here: 461 us
  Pallas kernels  429 us (93%)
  local copies, waits for them, and re-layouts  18.7 us (4%)
  other arithmetic  6.33 us (1%)
  starting transfers between devices  6.32 us (1%)
    pallas_call x1, Pallas kernels, select(): pl.pallas_call(select_kernel, out_shape=shapes, in_specs=[pl.BlockSpec(me...  192 us
    pallas_call x1, Pallas kernels, fetch(): pl.pallas_call(functools.partial(fetch_kernel, n_ctx, n_head, cuts), out_...  102 us
    pallas_call x1, Pallas kernels, forward(): pl.pallas_call(forward_kernel, grid_spec=pltpu.PrefetchScalarGridSpec(num...  38.6 us
    pallas_call x1, Pallas kernels, score_grads(): pl.pallas_call(functools.partial(grad_kernel, n_head), out_shape=jax.Shap...  37.1 us
    pallas_call x1, Pallas kernels, give_back(): pl.pallas_call(functools.partial(return_kernel, n_ctx, n_head), out_shape...  33 us
    pallas_call x1, Pallas kernels, backward(): pl.pallas_call(backward_kernel, grid_spec=pltpu.PrefetchScalarGridSpec(nu...  21.2 us
  transfers between devices with their start and end apart: 1, of which 0 were waited for; matrix products, arithmetic and copies ran while one was open for 3% of the time, Pallas kernels for 0%

profile of v2, /device:TPU:0, one launch (start us, length us, event | category | flops | bytes accessed | tf_op | source)
XLA Modules:
  0.0 461.4 jit_solution(7369669233628222891)
XLA Ops:
  0.6 0.8 copy.28
  1.4 0.1 eq.29
  1.5 1.9 fusion
  3.4 0.1 reshape.247
  3.5 0.1 reduce_sum.9
  3.6 0.2 reduce_window_sum.18
  3.9 0.2 reduce-window.8
  4.0 0.1 add.115
  4.1 0.1 add.116
  4.2 0.1 sub.44
  4.3 0.2 select_reduce_fusion
  4.5 0.7 all_to_all.6
  5.2 6.3 %all-to-all-start = ((s32[4,1,32]{2,1,0:T(1,128)}), s32[4,1,32]{2,1,0:T(1,128)S(1)}, u32[]{:S(2)}, u32[]{:S(2)}) async-start(s32[4,1,32]{2,1,0:T(1,128)} %bitcast.2), calls=%async_computation | async-start | bytes 4096 | tf_op jit(solution)/shard_map/all_to_all | solution.py:573
  11.5 0.1 reshape.227
  11.6 0.7 select_reduce_fusion.2
  12.3 0.9 compare_reduce_fusion
  13.2 0.7 multiply_bitcast_fusion
  13.9 0.1 reshape.243
  14.0 0.7 subtract_select_fusion.refs_20_
  14.7 0.6 constant_dynamic-slice_fusion
  15.3 0.6 max.17.own
  15.9 0.0 copy-start.1
  15.9 0.0 copy-start.2
  15.9 7.7 %copy.30 = bf16[4096,576]{1,0:T(8,128)(2,1)} copy(bf16[4096,576]{0,1:T(8,128)(2,1)} %param.9) | data formatting | bytes 9437184 | tf_op args[1]
  23.6 0.0 copy-done.1
  23.6 0.1 copy.31
  23.7 0.0 copy-start
  23.8 1.0 copy.32
  24.8 0.0 copy-done.2
  24.8 0.6 reshape.236.refs_19_.refs_10_
  25.4 0.6 reshape.238.refs_17_
  26.0 0.0 all-to-all-done
  26.0 0.5 broadcast.269
  26.5 0.7 reduce.9
  27.2 0.1 reshape.226
  27.3 0.7 max.15.mine
  28.0 192.4 %select.67 = (bf16[32,64,576]{2,1,0:T(8,128)(2,1)}, bf16[32,64,128]{2,1,0:T(8,128)(2,1)}, bf16[32,64,576]{2,1,0:T(8,128)(2,1)}, bf16[32,64,128]{2,1,0:T(8,128)(2,1)}) custom-call(s32[32]{0:T(128)} %max.15.mine, s32[32]{0:T(128)} %max.17.own, bf16[64,64,576]{2,1,0:T(8,128)(2,1)} %bitcast.55, bf16[64,64,128]{2,1,0:T(8,128)(2,1)} %bitcast.66), custom_call_target="tpu_custom_call" | custom-call | tf_op jit(solution)/shard_map/select/pallas_call | solution.py:160
  220.4 0.0 copy-done
  220.4 101.9 %fetch.1 = (bf16[4,4,8,64,576]{4,3,2,1,0:T(8,128)(2,1)}, bf16[4,4,8,64,128]{4,3,2,1,0:T(8,128)(2,1)}) custom-call(bf16[4,8,64,576]{3,2,1,0:T(8,128)(2,1)} %bitcast.62, bf16[4,8,64,128]{3,2,1,0:T(8,128)(2,1)} %bitcast.67, bf16[4,8,64,576]{3,2,1,0:T(8,128)(2,1)} %bitcast.63, bf16[4,8,64,128]{3,2,1,0:T(8,128)(2,1)} %bitcast.68), custom_call_target="tpu_custom_call" | custom-call | tf_op jit(solution)/shard_map/fetch/pallas_call | solution.py:117
  322.3 38.6 %forward.1 = (f32[4096,128]{1,0:T(8,128)}, f32[4096,128]{1,0:T(8,128)}) custom-call(s32[64]{0:T(128)} %get-tuple-element.28.src, bf16[128,64,576]{2,1,0:T(8,128)(2,1)} %bitcast.31, bf16[128,64,576]{2,1,0:T(8,128)(2,1)} %bitcast.32, bf16[128,64,576]{2,1,0:T(8,128)(2,1)} %bitcast.33, bf16[128,64,576]{2,1,0:T(8,128)(2,1)} %bitcast.34, ...), custom_call_target="tpu_custom_call" | custom-call | tf_op jit(solution)/shard_map/forward/pallas_call | solution.py:215
  360.9 37.1 %score_grads.1.refs_11_ = bf16[4096,128]{1,0:T(8,128)(2,1)} custom-call(f32[4096,128]{1,0:T(8,128)} %get-tuple-element.20.mass, f32[4096,128]{1,0:T(8,128)} %get-tuple-element.21.score, f32[1,128]{1,0:T(1,128)} %bitcast.76), custom_call_target="tpu_custom_call" | custom-call | tf_op jit(solution)/shard_map/score_grads/pallas_call | solution.py:318
  398.0 21.2 %backward.1 = (bf16[8,256,128]{2,1,0:T(8,128)(2,1)}, f32[8,256]{1,0:T(8,128)}, f32[4096,128]{1,0:T(8,128)}) custom-call(s32[64]{0:T(128)} %get-tuple-element.28.src, bf16[128,64,128]{2,1,0:T(8,128)(2,1)} %bitcast.47, bf16[128,64,128]{2,1,0:T(8,128)(2,1)} %bitcast.48, bf16[128,64,128]{2,1,0:T(8,128)(2,1)} %bitcast.49, bf16[128,64,128]{2,1,0:T(8,128)(2,1)} %bitcast.50, ...), custom_call_target="tpu_custom_call" | custom-call | tf_op jit(solution)/shard_map/backward/pallas_call | solution.py:382
  419.2 2.2 copy.35
  421.4 1.3 reshape.241
  422.7 0.6 reshape.242.asked
  423.3 33.0 %give_back.1 = bf16[4,4,8,64,128]{4,3,2,1,0:T(8,128)(2,1)} custom-call(s32[4,8]{1,0:T(4,128)} %bitcast.72, f32[4,16,64,128]{3,2,1,0:T(8,128)} %bitcast.65), custom_call_target="tpu_custom_call" | custom-call | tf_op jit(solution)/shard_map/give_back/pallas_call | solution.py:484
  456.3 5.1 %land.1 = f32[64,64,128]{2,1,0:T(8,128)} custom-call(s32[128]{0:T(128)} %reshape.242.asked, bf16[128,64,128]{2,1,0:T(8,128)(2,1)} %bitcast.56), custom_call_target="tpu_custom_call" | custom-call | tf_op jit(solution)/shard_map/land/pallas_call | solution.py:521
  (8 shorter events, 0.1 us)
Async XLA Ops:
  5.2 20.8 %all-to-all-start = ((s32[4,1,32]{2,1,0:T(1,128)}), s32[4,1,32]{2,1,0:T(1,128)S(1)}, u32[]{:S(2)}, u32[]{:S(2)}) async-start(s32[4,1,32]{2,1,0:T(1,128)} %bitcast.2), calls=%async_computation | async-start | bytes 4096 | tf_op jit(solution)/shard_map/all_to_all | solution.py:573
  15.9 7.7 %copy-start.1 = (bf16[128,16,128]{2,1,0:T(8,128)(2,1)S(1)}, bf16[128,16,128]{2,1,0:T(8,128)(2,1)}, u32[]{:S(2)}) copy-start(bf16[128,16,128]{2,1,0:T(8,128)(2,1)} %param.11) | copy-start | bytes 1572868
  15.9 8.9 %copy-start.2 = (f32[128,16]{0,1:T(8,128)S(1)}, f32[128,16]{0,1:T(8,128)}, u32[]{:S(2)}) copy-start(f32[128,16]{0,1:T(8,128)} %param.13) | copy-start | bytes 24580
  23.7 196.6 %copy-start = (bf16[128,16,128]{2,0,1:T(8,128)(2,1)}, bf16[128,16,128]{2,0,1:T(8,128)(2,1)S(1)}, u32[]{:S(2)}) copy-start(bf16[128,16,128]{2,0,1:T(8,128)(2,1)S(1)} %copy.31) | copy-start | bytes 1572868

commit v3 on v2

--- a/solution.py
+++ b/solution.py
@@ -120,7 +120,8 @@
             jax.ShapeDtypeStruct((n_ctx, n_head, per, BLK, wl), BF16),
             jax.ShapeDtypeStruct((n_ctx, n_head, per, BLK, wi), BF16),
         ),
-        in_specs=[pl.BlockSpec(memory_space=pl.ANY)] * 4,
+        in_specs=[pl.BlockSpec(memory_space=pl.ANY)] * 2
+        + [pl.BlockSpec(memory_space=pltpu.VMEM)] * 2,
         out_specs=(pl.BlockSpec(memory_space=pl.ANY),) * 2,
         scratch_shapes=[
             dma((2,)),
@@ -129,7 +130,9 @@
             dma((cuts + 1, n_ctx, n_x)),
             dma((cuts + 1, n_ctx, n_x)),
         ],
-        compiler_params=pltpu.CompilerParams(collective_id=0, has_side_effects=True),
+        compiler_params=pltpu.CompilerParams(
+            collective_id=0, has_side_effects=True, vmem_limit_bytes=VMEM_LIMIT
+        ),
         name="fetch",
     )(lat_mine, idx_mine, lat_own, idx_own)
 
@@ -161,8 +164,9 @@
         select_kernel,
         out_shape=shapes,
         in_specs=[pl.BlockSpec(memory_space=pltpu.SMEM)] * 2 + [anywhere] * 2,
-        out_specs=(anywhere,) * 4,
+        out_specs=(pl.BlockSpec(memory_space=pltpu.VMEM),) * 4,
         scratch_shapes=[pltpu.SemaphoreType.DMA((4,))],
+        compiler_params=pltpu.CompilerParams(vmem_limit_bytes=VMEM_LIMIT),
         name="select",
     )(mine, own, lat, idx)
 

time: 462 us -> 269 us (0.58)
  Pallas kernels: 429 us -> 236 us
    pallas_call x1, Pallas kernels: 192 us -> 9.63 us  [select(): pl.pallas_call(select_kernel, out_shape=shapes, in_specs=[pl.BlockSpec(me...]
    pallas_call x1, Pallas kernels: 102 us -> 89.3 us  [fetch(): pl.pallas_call(functools.partial(fetch_kernel, n_ctx, n_head, cuts), out_...]
  transfers between devices with their start and end apart: 1 -> 1, of which waited for: 0 -> 0; matrix products, arithmetic and copies ran while one was open for 3% -> 5% of each run, Pallas kernels for 0% -> 0%
where the time goes in v3:
time: 269 us; the launch traced here: 268 us
  Pallas kernels  236 us (88%)
  local copies, waits for them, and re-layouts  18.7 us (7%)
  other arithmetic  6.33 us (2%)
  starting transfers between devices  6.32 us (2%)
    pallas_call x1, Pallas kernels, fetch(): pl.pallas_call(functools.partial(fetch_kernel, n_ctx, n_head, cuts), out_...  89.3 us
    pallas_call x1, Pallas kernels, forward(): pl.pallas_call(forward_kernel, grid_spec=pltpu.PrefetchScalarGridSpec(num...  38.6 us
    pallas_call x1, Pallas kernels, score_grads(): pl.pallas_call(functools.partial(grad_kernel, n_head), out_shape=jax.Shap...  37.2 us
    pallas_call x1, Pallas kernels, give_back(): pl.pallas_call(functools.partial(return_kernel, n_ctx, n_head), out_shape...  35.4 us
    pallas_call x1, Pallas kernels, backward(): pl.pallas_call(backward_kernel, grid_spec=pltpu.PrefetchScalarGridSpec(nu...  21.2 us
    pallas_call x1, Pallas kernels, select(): pl.pallas_call(select_kernel, out_shape=shapes, in_specs=[pl.BlockSpec(me...  9.63 us
    unnamed x9, local copies, waits for them, and re-layouts  8.67 us
    all_to_all x1, starting transfers between devices, body(): lax.all_to_all(wanted.reshape(n_ctx, n_head * per), 'ctx', split_axis=0,...  6.32 us
  transfers between devices with their start and end apart: 1, of which 0 were waited for; matrix products, arithmetic and copies ran while one was open for 5% of the time, Pallas kernels for 0%

profile of v3, /device:TPU:0, one launch (start us, length us, event | category | flops | bytes accessed | tf_op | source)
XLA Modules:
  0.0 268.4 jit_solution(14342388393862516136)
XLA Ops:
  0.6 0.8 copy.28
  1.4 0.1 eq.29
  1.5 1.9 fusion
  3.4 0.1 reshape.247
  3.5 0.1 reduce_sum.9
  3.6 0.2 reduce_window_sum.18
  3.9 0.2 reduce-window.8
  4.0 0.1 add.115
  4.1 0.1 add.116
  4.2 0.1 sub.44
  4.3 0.2 select_reduce_fusion
  4.5 0.7 all_to_all.6
  5.2 6.3 %all-to-all-start = ((s32[4,1,32]{2,1,0:T(1,128)}), s32[4,1,32]{2,1,0:T(1,128)S(1)}, u32[]{:S(2)}, u32[]{:S(2)}) async-start(s32[4,1,32]{2,1,0:T(1,128)} %bitcast.2), calls=%async_computation | async-start | bytes 4096 | tf_op jit(solution)/shard_map/all_to_all | solution.py:577
  11.5 0.1 reshape.227
  11.6 0.7 select_reduce_fusion.2
  12.3 0.9 compare_reduce_fusion
  13.2 0.7 multiply_bitcast_fusion
  13.9 0.1 reshape.243
  14.0 0.7 subtract_select_fusion.refs_20_
  14.7 0.6 constant_dynamic-slice_fusion
  15.3 0.6 max.17.own
  15.9 0.0 copy-start.1
  15.9 0.0 copy-start.2
  15.9 7.7 %copy.30 = bf16[4096,576]{1,0:T(8,128)(2,1)} copy(bf16[4096,576]{0,1:T(8,128)(2,1)} %param.9) | data formatting | bytes 9437184 | tf_op args[1]
  23.6 0.0 copy-done.1
  23.6 0.1 copy.31
  23.7 0.0 copy-start
  23.8 1.0 copy.32
  24.8 0.0 copy-done.2
  24.8 0.6 reshape.236.refs_19_.refs_10_
  25.4 0.6 reshape.238.refs_17_
  26.0 0.0 all-to-all-done
  26.0 0.5 broadcast.269
  26.5 0.7 reduce.9
  27.2 0.1 reshape.226
  27.3 0.7 max.15.mine
  28.0 9.6 %select.67 = (bf16[32,64,576]{2,1,0:T(8,128)(2,1)}, bf16[32,64,128]{2,1,0:T(8,128)(2,1)}, bf16[32,64,576]{2,1,0:T(8,128)(2,1)}, bf16[32,64,128]{2,1,0:T(8,128)(2,1)}) custom-call(s32[32]{0:T(128)} %max.15.mine, s32[32]{0:T(128)} %max.17.own, bf16[64,64,576]{2,1,0:T(8,128)(2,1)} %bitcast.55, bf16[64,64,128]{2,1,0:T(8,128)(2,1)} %bitcast.66), custom_call_target="tpu_custom_call" | custom-call | tf_op jit(solution)/shard_map/select/pallas_call | solution.py:163
  37.6 0.0 copy-done
  37.6 89.3 %fetch.1 = (bf16[4,4,8,64,576]{4,3,2,1,0:T(8,128)(2,1)}, bf16[4,4,8,64,128]{4,3,2,1,0:T(8,128)(2,1)}) custom-call(bf16[4,8,64,576]{3,2,1,0:T(8,128)(2,1)} %bitcast.62, bf16[4,8,64,128]{3,2,1,0:T(8,128)(2,1)} %bitcast.67, bf16[4,8,64,576]{3,2,1,0:T(8,128)(2,1)} %bitcast.63, bf16[4,8,64,128]{3,2,1,0:T(8,128)(2,1)} %bitcast.68), custom_call_target="tpu_custom_call" | custom-call | tf_op jit(solution)/shard_map/fetch/pallas_call | solution.py:117
  126.9 38.6 %forward.1 = (f32[4096,128]{1,0:T(8,128)}, f32[4096,128]{1,0:T(8,128)}) custom-call(s32[64]{0:T(128)} %get-tuple-element.28.src, bf16[128,64,576]{2,1,0:T(8,128)(2,1)} %bitcast.31, bf16[128,64,576]{2,1,0:T(8,128)(2,1)} %bitcast.32, bf16[128,64,576]{2,1,0:T(8,128)(2,1)} %bitcast.33, bf16[128,64,576]{2,1,0:T(8,128)(2,1)} %bitcast.34, ...), custom_call_target="tpu_custom_call" | custom-call | tf_op jit(solution)/shard_map/forward/pallas_call | solution.py:219
  165.5 37.2 %score_grads.1.refs_11_ = bf16[4096,128]{1,0:T(8,128)(2,1)} custom-call(f32[4096,128]{1,0:T(8,128)} %get-tuple-element.20.mass, f32[4096,128]{1,0:T(8,128)} %get-tuple-element.21.score, f32[1,128]{1,0:T(1,128)} %bitcast.76), custom_call_target="tpu_custom_call" | custom-call | tf_op jit(solution)/shard_map/score_grads/pallas_call | solution.py:322
  202.7 21.2 %backward.1 = (bf16[8,256,128]{2,1,0:T(8,128)(2,1)}, f32[8,256]{1,0:T(8,128)}, f32[4096,128]{1,0:T(8,128)}) custom-call(s32[64]{0:T(128)} %get-tuple-element.28.src, bf16[128,64,128]{2,1,0:T(8,128)(2,1)} %bitcast.47, bf16[128,64,128]{2,1,0:T(8,128)(2,1)} %bitcast.48, bf16[128,64,128]{2,1,0:T(8,128)(2,1)} %bitcast.49, bf16[128,64,128]{2,1,0:T(8,128)(2,1)} %bitcast.50, ...), custom_call_target="tpu_custom_call" | custom-call | tf_op jit(solution)/shard_map/backward/pallas_call | solution.py:386
  223.9 2.2 copy.35
  226.1 1.3 reshape.241
  227.4 0.6 reshape.242.asked
  228.0 35.4 %give_back.1 = bf16[4,4,8,64,128]{4,3,2,1,0:T(8,128)(2,1)} custom-call(s32[4,8]{1,0:T(4,128)} %bitcast.72, f32[4,16,64,128]{3,2,1,0:T(8,128)} %bitcast.65), custom_call_target="tpu_custom_call" | custom-call | tf_op jit(solution)/shard_map/give_back/pallas_call | solution.py:488
  263.4 5.0 %land.1 = f32[64,64,128]{2,1,0:T(8,128)} custom-call(s32[128]{0:T(128)} %reshape.242.asked, bf16[128,64,128]{2,1,0:T(8,128)(2,1)} %bitcast.56), custom_call_target="tpu_custom_call" | custom-call | tf_op jit(solution)/shard_map/land/pallas_call | solution.py:525
  (8 shorter events, 0.1 us)
Async XLA Ops:
  5.2 20.8 %all-to-all-start = ((s32[4,1,32]{2,1,0:T(1,128)}), s32[4,1,32]{2,1,0:T(1,128)S(1)}, u32[]{:S(2)}, u32[]{:S(2)}) async-start(s32[4,1,32]{2,1,0:T(1,128)} %bitcast.2), calls=%async_computation | async-start | bytes 4096 | tf_op jit(solution)/shard_map/all_to_all | solution.py:577
  15.9 7.7 %copy-start.1 = (bf16[128,16,128]{2,1,0:T(8,128)(2,1)S(1)}, bf16[128,16,128]{2,1,0:T(8,128)(2,1)}, u32[]{:S(2)}) copy-start(bf16[128,16,128]{2,1,0:T(8,128)(2,1)} %param.11) | copy-start | bytes 1572868
  15.9 8.9 %copy-start.2 = (f32[128,16]{0,1:T(8,128)S(1)}, f32[128,16]{0,1:T(8,128)}, u32[]{:S(2)}) copy-start(f32[128,16]{0,1:T(8,128)} %param.13) | copy-start | bytes 24580
  23.7 13.9 %copy-start = (bf16[128,16,128]{2,0,1:T(8,128)(2,1)}, bf16[128,16,128]{2,0,1:T(8,128)(2,1)S(1)}, u32[]{:S(2)}) copy-start(bf16[128,16,128]{2,0,1:T(8,128)(2,1)S(1)} %copy.31) | copy-start | bytes 1572868

commit v4 on v3

--- a/solution.py
+++ b/solution.py
@@ -11,6 +11,8 @@
 BLK = 64
 UB = 64
 GB = 8
+CUTS = 4
+AHEAD = 2
 ATTN_SCALE = 192.0 ** (-0.5)
 LOG2E = math.log2(math.e)
 MESH = pl.DeviceIdType.MESH
@@ -58,12 +60,15 @@
         return idx_got.at[o, h] if a == 0 else lat_got.at[o, h, pl.ds((a - 1) * piece, piece)]
 
     pending = []
-    for a in units:
+    def outward(a):
         for i, o in enumerate(others):
             c = remote(mine(a, o), got(a, me, head), s_ctx.at[a, i],
                        recv_sem.at[a, me, head], {"ctx": o})
             c.start()
             pending.append(c)
+
+    for a in units[:AHEAD]:
+        outward(a)
     locals_ = [
         pltpu.make_async_copy(idx_own, idx_got.at[me], own_sem.at[0]),
         pltpu.make_async_copy(lat_own, lat_got.at[me], own_sem.at[1]),
@@ -95,6 +100,8 @@
 
     for a in units:
         across(a)
+        if a + AHEAD <= cuts:
+            outward(a + AHEAD)
         if a > 0:
             along(a - 1)
     along(cuts)
@@ -109,16 +116,15 @@
 
 
 def fetch(n_ctx, n_head, lat_mine, idx_mine, lat_own, idx_own):
-    per, _, wl = lat_mine.shape[1:]
-    wi = idx_mine.shape[-1]
+    per = lat_mine.shape[1]
     n_x = n_head // 2
-    cuts = math.gcd(per, 4)
+    cuts = math.gcd(per, CUTS)
     dma = pltpu.SemaphoreType.DMA
     return pl.pallas_call(
         functools.partial(fetch_kernel, n_ctx, n_head, cuts),
         out_shape=(
-            jax.ShapeDtypeStruct((n_ctx, n_head, per, BLK, wl), BF16),
-            jax.ShapeDtypeStruct((n_ctx, n_head, per, BLK, wi), BF16),
+            jax.ShapeDtypeStruct((n_ctx, n_head) + lat_mine.shape[1:], BF16),
+            jax.ShapeDtypeStruct((n_ctx, n_head) + idx_mine.shape[1:], BF16),
         ),
         in_specs=[pl.BlockSpec(memory_space=pl.ANY)] * 2
         + [pl.BlockSpec(memory_space=pltpu.VMEM)] * 2,
@@ -176,9 +182,13 @@
     idx = refs[GB:2 * GB]
     mq, lse, iq, hw, lim, mass, score, keys, ikeys = refs[2 * GB:]
     q = mass.shape[1]
+    wide = lat[0].shape[-1]
     for b in range(GB):
-        keys[b * BLK:(b + 1) * BLK, :] = lat[b][0]
-        ikeys[b * BLK:(b + 1) * BLK, :] = idx[b][0]
+        low, mid, high = b * BLK, b * BLK + BLK // 2, (b + 1) * BLK
+        keys[low:high, :wide] = lat[b][0]
+        keys[low:mid, wide:] = idx[b][0, BLK:, :BLK]
+        keys[mid:high, wide:] = idx[b][0, BLK:, BLK:]
+        ikeys[low:high, :] = idx[b][0, :BLK, :]
     mass[...] = jnp.zeros_like(mass)
     score[...] = jnp.zeros_like(score)
 
@@ -205,15 +215,15 @@
         score[rows, :] = jnp.where(seen, score[rows, :], -1e30)
 
 
-def slot_specs(width):
+def slot_specs(array):
     return [
-        pl.BlockSpec((1, BLK, width), lambda g, s, b=b: (s[g * GB + b], 0, 0)) for b in range(GB)
+        pl.BlockSpec((1,) + array.shape[1:], lambda g, s, b=b: (s[g * GB + b], 0, 0)) for b in range(GB)
     ]
 
 
 def forward(source, lat, idx, mq, lse, iq, hw, lim):
     q = lim.shape[1]
-    wl, wi = lat.shape[-1], idx.shape[-1]
+    wl, wi = mq.shape[1], idx.shape[-1]
     rows = GB * BLK
     whole = lambda a: pl.BlockSpec(a.shape, lambda g, s, n=a.ndim: (0,) * n)
     return pl.pallas_call(
@@ -221,7 +231,7 @@
         grid_spec=pltpu.PrefetchScalarGridSpec(
             num_scalar_prefetch=1,
             grid=(UB // GB,),
-            in_specs=slot_specs(wl) + slot_specs(wi) + [whole(mq), whole(lse), whole(iq), whole(hw)]
+            in_specs=slot_specs(lat) + slot_specs(idx) + [whole(mq), whole(lse), whole(iq), whole(hw)]
             + [pl.BlockSpec((GB, q), lambda g, s: (g, 0))],
             out_specs=(pl.BlockSpec((rows, q), lambda g, s: (g, 0)),) * 2,
             scratch_shapes=[pltpu.VMEM((rows, wl), BF16), pltpu.VMEM((rows, wi), BF16)],
@@ -354,7 +364,7 @@
         dw[...] = jnp.zeros_like(dw)
 
     for b in range(GB):
-        ikeys[b * BLK:(b + 1) * BLK, :] = idx[b][0]
+        ikeys[b * BLK:(b + 1) * BLK, :] = idx[b][0, :BLK, :]
     tkeys[...] = jnp.swapaxes(ikeys[...].astype(F32), 0, 1).astype(BF16)
     gacc[...] = jnp.zeros_like(gacc)
 
@@ -388,7 +398,7 @@
         grid_spec=pltpu.PrefetchScalarGridSpec(
             num_scalar_prefetch=1,
             grid=(UB // GB,),
-            in_specs=slot_specs(wi) + [whole(iq), whole(iqt), whole(hw), pl.BlockSpec((rows, q), lambda g, s: (g, 0))],
+            in_specs=slot_specs(idx) + [whole(iq), whole(iqt), whole(hw), pl.BlockSpec((rows, q), lambda g, s: (g, 0))],
             out_specs=(
                 pl.BlockSpec((pairs, 2 * q, wi), lambda g, s: (0, 0, 0)),
                 pl.BlockSpec((pairs, 2 * q), lambda g, s: (0, 0)),
@@ -577,8 +587,13 @@
     asked = lax.all_to_all(
         wanted.reshape(n_ctx, n_head * per), "ctx", split_axis=0, concat_axis=0, tiled=True
     )
-    lat_local = latent_keys.reshape(owner_blocks, BLK, wl)
-    idx_local = index_keys.reshape(owner_blocks, BLK, wi)
+    wide = wl - BLK
+    lat_local = latent_keys[:, :wide].reshape(owner_blocks, BLK, wide)
+    tail = latent_keys[:, wide:].reshape(owner_blocks, 2, BLK // 2, BLK).transpose(0, 2, 1, 3)
+    idx_local = jnp.concatenate(
+        [index_keys.reshape(owner_blocks, BLK, wi), tail.reshape(owner_blocks, BLK // 2, 2 * BLK)],
+        axis=1,
+    )
     want3 = wanted.reshape(n_ctx, n_head, per)
     ask3 = asked.reshape(n_ctx, n_head, per)
     mine = jnp.maximum(lax.dynamic_index_in_dim(ask3, head, 1, keepdims=False), 0)
@@ -590,13 +605,13 @@
     lat_got, idx_got = fetch(
         n_ctx,
         n_head,
-        lat_mine.reshape(n_ctx, per, BLK, wl),
-        idx_mine.reshape(n_ctx, per, BLK, wi),
-        lat_own.reshape(n_head, per, BLK, wl),
-        idx_own.reshape(n_head, per, BLK, wi),
-    )
-    lat_got = lat_got.reshape(n_slot, BLK, wl)
-    idx_got = idx_got.reshape(n_slot, BLK, wi)
+        lat_mine.reshape((n_ctx, per) + lat_mine.shape[1:]),
+        idx_mine.reshape((n_ctx, per) + idx_mine.shape[1:]),
+        lat_own.reshape((n_head, per) + lat_own.shape[1:]),
+        idx_own.reshape((n_head, per) + idx_own.shape[1:]),
+    )
+    lat_got = lat_got.reshape((n_slot,) + lat_got.shape[3:])
+    idx_got = idx_got.reshape((n_slot,) + idx_got.shape[3:])
     chosen = jnp.any(union_block[:, None, None] == block_ids[None, :, :], axis=2)
     query_pos = all_blocks * BLK - q * n_ctx + me * q + jnp.arange(q, dtype=jnp.int32)
     lim = jnp.where(chosen, query_pos[None, :] - union_block[:, None] * BLK, -1)

time: 269 us -> 269 us (level)
  Pallas kernels: 236 us -> 228 us
  local copies, waits for them, and re-layouts: 18.7 us -> 25.3 us
    pallas_call x1, Pallas kernels: 89.3 us -> 76.2 us  [fetch(): pl.pallas_call(functools.partial(fetch_kernel, n_ctx, n_head, cuts), out_...]
    slice x0 -> x3, local copies, waits for them, and re-layouts: none -> 12.3 us  [the longest x2 11.2 us: body(): lat_local = latent_keys[:, :wide].reshape(owner_blocks, BLK, wide)]
    unnamed x9 -> x13, local copies, waits for them, and re-layouts: 8.67 us -> 1.45 us
    pallas_call x1, Pallas kernels: 35.4 us -> 41.6 us  [give_back(): pl.pallas_call(functools.partial(return_kernel, n_ctx, n_head), out_shape...]
  transfers between devices with their start and end apart: 1 -> 1, of which waited for: 0 -> 0; matrix products, arithmetic and copies ran while one was open for 5% -> 8% of each run, Pallas kernels for 0% -> 0%
where the time goes in v4:
time: 269 us; the launch traced here: 268 us
  Pallas kernels  228 us (85%)
  local copies, waits for them, and re-layouts  25.3 us (9%)
  other arithmetic  7.01 us (3%)
  starting transfers between devices  6.32 us (2%)
    pallas_call x1, Pallas kernels, fetch(): pl.pallas_call(functools.partial(fetch_kernel, n_ctx, n_head, cuts), out_...  76.2 us
    pallas_call x1, Pallas kernels, give_back(): pl.pallas_call(functools.partial(return_kernel, n_ctx, n_head), out_shape...  41.6 us
    pallas_call x1, Pallas kernels, forward(): pl.pallas_call(forward_kernel, grid_spec=pltpu.PrefetchScalarGridSpec(num...  38.5 us
    pallas_call x1, Pallas kernels, score_grads(): pl.pallas_call(functools.partial(grad_kernel, n_head), out_shape=jax.Shap...  37.1 us
    pallas_call x1, Pallas kernels, backward(): pl.pallas_call(backward_kernel, grid_spec=pltpu.PrefetchScalarGridSpec(nu...  21.2 us
    slice x2, local copies, waits for them, and re-layouts, body(): lat_local = latent_keys[:, :wide].reshape(owner_blocks, BLK, wide)  11.2 us
    pallas_call x1, Pallas kernels, select(): pl.pallas_call(select_kernel, out_shape=shapes, in_specs=[pl.BlockSpec(me...  8.46 us
    all_to_all x1, starting transfers between devices, body(): lax.all_to_all(wanted.reshape(n_ctx, n_head * per), 'ctx', split_axis=0,...  6.32 us
  transfers between devices with their start and end apart: 1, of which 0 were waited for; matrix products, arithmetic and copies ran while one was open for 8% of the time, Pallas kernels for 0%

profile of v4, /device:TPU:0, one launch (start us, length us, event | category | flops | bytes accessed | tf_op | source)
XLA Modules:
  0.0 267.6 jit_solution(1565375948767401627)
XLA Ops:
  0.6 0.8 copy.33
  1.4 0.1 eq.29
  1.5 1.9 fusion
  3.4 0.1 reshape.255
  3.5 0.1 reduce_sum.9
  3.6 0.2 reduce_window_sum.18
  3.9 0.2 reduce-window.8
  4.0 0.1 add.115
  4.1 0.1 add.116
  4.2 0.1 sub.44
  4.3 0.2 select_reduce_fusion
  4.5 0.7 all_to_all.6
  5.2 6.3 %all-to-all-start = ((s32[4,1,32]{2,1,0:T(1,128)}), s32[4,1,32]{2,1,0:T(1,128)S(1)}, u32[]{:S(2)}, u32[]{:S(2)}) async-start(s32[4,1,32]{2,1,0:T(1,128)} %bitcast.2), calls=%async_computation | async-start | bytes 4096 | tf_op jit(solution)/shard_map/all_to_all | solution.py:587
  11.5 0.1 reshape.233
  11.6 0.7 select_reduce_fusion.2
  12.3 0.9 compare_reduce_fusion
  13.2 0.0 copy-start.3
  13.3 0.0 copy-start.1
  13.3 1.2 slice.7
  14.4 0.5 copy.41
  14.9 1.1 copy.37
  16.0 0.5 reshape.237
  16.5 0.0 copy-done.3
  16.5 0.1 reshape.251
  16.6 0.0 copy-done.1
  16.7 1.3 pad_maximum_fusion.idx
  18.0 0.7 subtract_select_fusion.refs_20_
  18.7 0.6 constant_dynamic-slice_fusion
  19.3 4.7 %slice.6 = bf16[4096,512]{0,1:T(8,128)(2,1)} slice(bf16[4096,576]{0,1:T(8,128)(2,1)} %param.9), slice={[0:4096], [0:512]} | slice | bytes 8388608 | tf_op jit(solution)/shard_map/slice | solution.py:591
  23.9 0.6 max.17.own
  24.5 0.0 copy-start.2
  24.5 0.0 copy-start.4
  24.5 6.5 %copy.35 = bf16[4096,512]{1,0:T(8,128)(2,1)} copy(bf16[4096,512]{0,1:T(8,128)(2,1)} %slice.6) | data formatting | bytes 8388608 | tf_op jit(solution)/shard_map/slice | solution.py:591
  31.0 0.0 copy-done.2
  31.0 0.1 copy.38
  31.1 0.0 copy-start
  31.2 1.0 copy.39
  32.2 0.0 copy-done.4
  32.2 0.6 reshape.244.refs_19_.refs_10_
  32.8 0.6 reshape.246.refs_17_
  33.4 0.0 all-to-all-done
  33.4 0.5 broadcast.269
  33.9 0.7 reduce.9
  34.6 0.1 reshape.232
  34.7 0.6 max.15.mine
  35.3 8.5 %select.67 = (bf16[32,64,512]{2,1,0:T(8,128)(2,1)}, bf16[32,96,128]{2,1,0:T(8,128)(2,1)}, bf16[32,64,512]{2,1,0:T(8,128)(2,1)}, bf16[32,96,128]{2,1,0:T(8,128)(2,1)}) custom-call(s32[32]{0:T(128)} %max.15.mine, s32[32]{0:T(128)} %max.17.own, bf16[64,64,512]{2,1,0:T(8,128)(2,1)} %bitcast.58, bf16[64,96,128]{2,1,0:T(8,128)(2,1)} %pad_maximum_fusion.idx), custom_call_target="tpu_custom_call" | custom-call | tf_op jit(solution)/shard_map/select/pallas_call | solution.py:169
  43.8 0.0 copy-done
  43.8 76.2 %fetch.1 = (bf16[4,4,8,64,512]{4,3,2,1,0:T(8,128)(2,1)}, bf16[4,4,8,96,128]{4,3,2,1,0:T(8,128)(2,1)}) custom-call(bf16[4,8,64,512]{3,2,1,0:T(8,128)(2,1)} %bitcast.68, bf16[4,8,96,128]{3,2,1,0:T(8,128)(2,1)} %bitcast.71, bf16[4,8,64,512]{3,2,1,0:T(8,128)(2,1)} %bitcast.69, bf16[4,8,96,128]{3,2,1,0:T(8,128)(2,1)} %bitcast.72), custom_call_target="tpu_custom_call" | custom-call | tf_op jit(solution)/shard_map/fetch/pallas_call | solution.py:123
  120.0 38.5 %forward.1 = (f32[4096,128]{1,0:T(8,128)}, f32[4096,128]{1,0:T(8,128)}) custom-call(s32[64]{0:T(128)} %get-tuple-element.28.src, bf16[128,64,512]{2,1,0:T(8,128)(2,1)} %bitcast.50, bf16[128,64,512]{2,1,0:T(8,128)(2,1)} %bitcast.51, bf16[128,64,512]{2,1,0:T(8,128)(2,1)} %bitcast.52, bf16[128,64,512]{2,1,0:T(8,128)(2,1)} %bitcast.53, ...), custom_call_target="tpu_custom_call" | custom-call | tf_op jit(solution)/shard_map/forward/pallas_call | solution.py:229
  158.5 37.1 %score_grads.1.refs_11_ = bf16[4096,128]{1,0:T(8,128)(2,1)} custom-call(f32[4096,128]{1,0:T(8,128)} %get-tuple-element.20.mass, f32[4096,128]{1,0:T(8,128)} %get-tuple-element.21.score, f32[1,128]{1,0:T(1,128)} %bitcast.80), custom_call_target="tpu_custom_call" | custom-call | tf_op jit(solution)/shard_map/score_grads/pallas_call | solution.py:332
  195.6 21.2 %backward.1 = (bf16[8,256,128]{2,1,0:T(8,128)(2,1)}, f32[8,256]{1,0:T(8,128)}, f32[4096,128]{1,0:T(8,128)}) custom-call(s32[64]{0:T(128)} %get-tuple-element.28.src, bf16[128,96,128]{2,1,0:T(8,128)(2,1)} %bitcast.42, bf16[128,96,128]{2,1,0:T(8,128)(2,1)} %bitcast.43, bf16[128,96,128]{2,1,0:T(8,128)(2,1)} %bitcast.44, bf16[128,96,128]{2,1,0:T(8,128)(2,1)} %bitcast.45, ...), custom_call_target="tpu_custom_call" | custom-call | tf_op jit(solution)/shard_map/backward/pallas_call | solution.py:396
  216.8 2.2 copy.43
  219.0 1.3 reshape.249
  220.3 0.6 reshape.250.asked
  220.9 41.6 %give_back.1 = bf16[4,4,8,64,128]{4,3,2,1,0:T(8,128)(2,1)} custom-call(s32[4,8]{1,0:T(4,128)} %bitcast.76, f32[4,16,64,128]{3,2,1,0:T(8,128)} %bitcast.67), custom_call_target="tpu_custom_call" | custom-call | tf_op jit(solution)/shard_map/give_back/pallas_call | solution.py:498
  262.5 5.0 %land.1 = f32[64,64,128]{2,1,0:T(8,128)} custom-call(s32[128]{0:T(128)} %reshape.250.asked, bf16[128,64,128]{2,1,0:T(8,128)(2,1)} %bitcast.59), custom_call_target="tpu_custom_call" | custom-call | tf_op jit(solution)/shard_map/land/pallas_call | solution.py:535
  (9 shorter events, 0.1 us)
Async XLA Ops:
  5.2 28.2 %all-to-all-start = ((s32[4,1,32]{2,1,0:T(1,128)}), s32[4,1,32]{2,1,0:T(1,128)S(1)}, u32[]{:S(2)}, u32[]{:S(2)}) async-start(s32[4,1,32]{2,1,0:T(1,128)} %bitcast.2), calls=%async_computation | async-start | bytes 4096 | tf_op jit(solution)/shard_map/all_to_all | solution.py:587
  13.2 3.3 %copy-start.3 = (f32[128,32]{0,1:T(8,128)S(1)}, f32[128,32]{0,1:T(8,128)}, u32[]{:S(2)}) copy-start(f32[128,32]{0,1:T(8,128)} %param.10) | copy-start | bytes 49156
  13.3 3.4 %copy-start.1 = (bf16[4096,128]{1,0:T(8,128)(2,1)S(1)}, bf16[4096,128]{1,0:T(8,128)(2,1)}, u32[]{:S(2)}) copy-start(bf16[4096,128]{1,0:T(8,128)(2,1)} %param.12) | copy-start | bytes 3145732
  24.5 6.5 %copy-start.2 = (bf16[128,16,128]{2,1,0:T(8,128)(2,1)S(1)}, bf16[128,16,128]{2,1,0:T(8,128)(2,1)}, u32[]{:S(2)}) copy-start(bf16[128,16,128]{2,1,0:T(8,128)(2,1)} %param.11) | copy-start | bytes 1572868
  24.5 7.7 %copy-start.4 = (f32[128,16]{0,1:T(8,128)S(1)}, f32[128,16]{0,1:T(8,128)}, u32[]{:S(2)}) copy-start(f32[128,16]{0,1:T(8,128)} %param.13) | copy-start | bytes 24580
  31.1 12.6 %copy-start = (bf16[128,16,128]{2,0,1:T(8,128)(2,1)}, bf16[128,16,128]{2,0,1:T(8,128)(2,1)S(1)}, u32[]{:S(2)}) copy-start(bf16[128,16,128]{2,0,1:T(8,128)(2,1)S(1)} %copy.38) | copy-start | bytes 1572868
